TPU v7x, 256 devices: a whole 4x4x8 slice. The times are simulated.
256 devices in a mesh: dp: 4 (over z_hi), ctx: 16 (over x, y), head: 4 (over z_lo, core).
Axes of the slice: x: 4, y: 4, z: 8 (z_hi: 4, z_lo: 2; z = z_hi * 2 + z_lo), core: 2. Of those that a mesh axis runs over, the one named last changes fastest.
Arguments:
- queries: bfloat16 [4, 2048, 64, 288], P('dp', 'ctx', 'head'), may hold values from -100 to 100
- latents: bfloat16 [4, 2048, 288], P('dp', 'ctx'), may hold values from -16 to 16
- positions: int32 [4, 2048], P('dp', 'ctx'), may hold values from 0 to 2047, as said below
- lse: float32 [4, 2048, 64], P('dp', 'ctx', 'head'), as said below
- saved_out: bfloat16 [4, 2048, 64, 256], P('dp', 'ctx', 'head'), may hold values from -6 to 6
- out_grad: bfloat16 [4, 2048, 64, 128], P('dp', 'ctx', 'head'), may hold values from -6 to 6
- value_up: bfloat16 [64, 256, 128], P('head'), may hold values from -0.375 to 0.375
Outputs:
- query_grad: bfloat16 [4, 2048, 64, 288], P('dp', 'ctx', 'head')
- latent_grad: float32 [4, 2048, 288], P('dp', 'ctx')
- value_up_grad: float32 [256, 64, 128], P(('dp', 'ctx'), 'head')
Inputs may be any that keep to these rules, and one draw needn't show every extreme that they name: For each sequence the 2048 positions are a permutation of 0 to 2047; the 128 slots of each aligned block of 128 slots hold 128 consecutive positions, beginning at a multiple of 128, in some order. lse[b, i, h] is the logarithm of the sum over the slots j visible to i of exp(logits[i, j]).
All inputs are finite; a program needn't handle non-finite values.
Results may differ from a plain program's by a relative error of at most 0.014.
Values may be sent and summed in bfloat16 or wider, within the bound.
No kernel may reach another device: no remote copies, remote signals or barrier semaphores. Data moves between devices by JAX's collectives and lax.ppermute only.
A program may use at most 64 MiB of HBM per device.

v0:
```python
import jax
import jax.numpy as jnp
from jax import lax
from jax.sharding import PartitionSpec as P

ROPE = 32
VHEAD = 128


def spans(length):
    return [(lower, min(length, lower + 512)) for lower in range(0, length, 512)]


def body(queries, latents, positions, lse, saved_out, out_grad, value_up):
    query_rows = queries[0]
    slot_count = query_rows.shape[0]
    head_count = query_rows.shape[1]
    full_width = query_rows.shape[2]
    latent_width = saved_out.shape[3]
    query_pos = positions[0]
    row_lse = lse[0]
    latest = jnp.max(query_pos)
    scaling = (VHEAD + ROPE) ** (-0.5)
    lat_grad = jnp.einsum(
        "thv,hlv->thl", out_grad[0], value_up, preferred_element_type=jnp.float32
    ).astype(jnp.bfloat16)
    row_delta = jnp.sum(lat_grad.astype(jnp.float32) * saved_out[0].astype(jnp.float32), axis=-1)
    slab_rows = slot_count * lax.axis_size("ctx")
    grad_init = (
        jnp.zeros((slot_count, head_count, full_width), jnp.float32),
        jnp.zeros((slab_rows, full_width), jnp.float32),
    )
    carry = grad_init
    keys_in = lax.all_gather(latents[0], "ctx", axis=0, tiled=True)
    pos_in = lax.all_gather(positions[0], "ctx", axis=0, tiled=True)
    for lower, upper in spans(keys_in.shape[0]):
        key_rows = keys_in[lower:upper]
        key_pos = pos_in[lower:upper]

        def update(state):
            query_acc, key_acc = state
            logits = (
                jnp.einsum("thd,kd->thk", query_rows, key_rows, preferred_element_type=jnp.float32)
                * scaling
            )
            visible = key_pos[None, None, :] <= query_pos[:, None, None]
            weights = jnp.where(visible, jnp.exp(logits - row_lse[:, :, None]), 0.0)
            dot_value = jnp.einsum(
                "thl,kl->thk",
                lat_grad,
                key_rows[:, :latent_width],
                preferred_element_type=jnp.float32,
            )
            dlogits = (weights * (dot_value - row_delta[:, :, None]) * scaling).astype(jnp.bfloat16)
            query_acc = query_acc + jnp.einsum(
                "thk,kd->thd", dlogits, key_rows, preferred_element_type=jnp.float32
            )
            key_term = jnp.einsum(
                "thk,thd->kd", dlogits, query_rows, preferred_element_type=jnp.float32
            )
            value_term = jnp.einsum(
                "thk,thl->kl",
                weights.astype(jnp.bfloat16),
                lat_grad,
                preferred_element_type=jnp.float32,
            )
            key_term = key_term + jnp.pad(value_term, ((0, 0), (0, full_width - latent_width)))
            previous = lax.dynamic_slice_in_dim(key_acc, 0 + lower, upper - lower, 0)
            key_acc = lax.dynamic_update_slice_in_dim(key_acc, previous + key_term, 0 + lower, 0)
            return (query_acc, key_acc)

        carry = lax.cond(jnp.min(key_pos) > latest, lambda state: state, update, carry)
    query_acc, key_acc = carry
    summed = lax.psum(key_acc, "head")
    own_rows = lax.psum_scatter(summed, "ctx", scatter_dimension=0, tiled=True)
    saved_part = saved_out[0]
    weight_share = lax.psum_scatter(
        jnp.einsum("thl,thv->lhv", saved_part, out_grad[0], preferred_element_type=jnp.float32),
        ("dp", "ctx"),
        scatter_dimension=0,
        tiled=True,
    )
    return (query_acc.astype(jnp.bfloat16)[None], own_rows[None], weight_share)


def solution(mesh):
    return jax.shard_map(
        body,
        mesh=mesh,
        in_specs=(
            P("dp", "ctx", "head", None),
            P("dp", "ctx", None),
            P("dp", "ctx"),
            P("dp", "ctx", "head"),
            P("dp", "ctx", "head", None),
            P("dp", "ctx", "head", None),
            P("head", None, None),
        ),
        out_specs=(
            P("dp", "ctx", "head", None),
            P("dp", "ctx", None),
            P(("dp", "ctx"), "head", None),
        ),
        check_vma=False,
    )
```

profile of v0, /device:TPU:1, one launch (start us, length us, event | category | flops | bytes accessed | tf_op | source)
XLA Modules:
  0.0 624.3 jit_solution(3675719398537834552)
XLA Ops:
  8.0 1.4 reduce_max.9
  9.3 17.2 %all-gather = s32[1,2048]{1,0:T(1,128)S(1)} all-gather(s32[1,128]{1,0:T(1,128)} %param.17), channel_id=2, replica_groups=mesh['dp'=4,'ctx'=16,'head'=4] {'ctx'}, dimensions={1}, use_global_device_ids=true | all-gather | bytes 8704 | tf_op jit(solution)/shard_map/all_gather | solution.py:35
  32.6 1.5 copy.45
  34.1 2.9 copy.41
  36.9 2.8 multiply_reduce_fusion
  39.7 22.2 %all-gather.4.cloned.1.call-done = bf16[1,2048,288]{1,2,0:T(8,128)(2,1)} async-done(((bf16[1,128,288]{1,2,0:T(8,128)(2,1)}), bf16[1,2048,288]{1,2,0:T(8,128)(2,1)}) %all-gather.4.cloned.1.call-update) | async-done | bytes 1179664 | tf_op jit(solution)/shard_map/all_gather | solution.py:34
  61.9 2.0 slice_bitcast_fusion.8
  63.9 8.4 %conditional.4 = (f32[128,16,288]{0,2,1:T(8,128)S(1)}, f32[2048,288]{0,1:T(8,128)}) conditional(s32[]{:T(128)} %convert_element_type.67, (s32[512]{0:T(512)S(1)}, s32[1,128]{1,0:T(1,128)S(1)}, bf16[128,16,288]{0,2,1:T(8,128)(2,1)S(1)}, bf16[512,288]{0,1:T(8,128)(2,1)S(1)}, f32[1,128,16]{1,2,0:T(8,128)S(1)}, ...), branch_computations={%region_6.7_spmd, %region_7.8_spmd} | conditional | flops 2897428480 | bytes 38496872 | solution.py:72
  66.6 2.2 multiply_convert_fusion
  70.6 1.7 dynamic_update_slice.8
  72.3 11.7 %conditional.5 = ((f32[128,16,288]{0,2,1:T(8,128)S(1)}, f32[2048,288]{0,1:T(8,128)})) conditional(s32[]{:T(128)} %convert_element_type.66, (s32[512]{0:T(512)S(1)}, s32[1,128]{1,0:T(1,128)S(1)}, bf16[128,16,288]{0,2,1:T(8,128)(2,1)}, bf16[512,288]{0,1:T(8,128)(2,1)}, f32[1,128,16]{1,2,0:T(8,128)S(1)}, /*index=5*/bf16[128,16,256]{0,2,1:T(8,128)(2,1)}, ...), branch_computations={%region_8.9_spmd, %region_9.10_spmd} | conditional | flops 2898165760 | bytes 43215496 | solution.py:72
  72.4 1.9 copy.43
  74.3 2.7 fusion.31
  78.1 2.1 multiply_convert_fusion.1
  80.2 2.7 fusion.29
  84.0 11.9 %conditional.6 = ((f32[128,16,288]{0,2,1:T(8,128)S(1)}, f32[2048,288]{0,1:T(8,128)})) conditional(s32[]{:T(128)} %convert_element_type.61, (s32[512]{0:T(512)S(1)}, s32[1,128]{1,0:T(1,128)S(1)}, bf16[128,16,288]{0,2,1:T(8,128)(2,1)}, bf16[512,288]{0,1:T(8,128)(2,1)}, f32[1,128,16]{1,2,0:T(8,128)S(1)}, /*index=5*/bf16[128,16,256]{0,2,1:T(8,128)(2,1)}, ...), branch_computations={%region_10.11_spmd, %region_11.12_spmd} | conditional | flops 2898165760 | bytes 43215496 | solution.py:72
  84.3 1.9 copy.44
  86.2 2.7 fusion.49
  90.0 2.1 multiply_convert_fusion.2
  92.1 2.7 fusion.47
  95.9 15.2 %conditional.7 = (f32[2048,288]{0,1:T(8,128)}, bf16[1,128,16,288]{1,3,2,0:T(8,128)(2,1)}) conditional(s32[]{:T(128)} %convert_element_type.60, (f32[2048,288]{0,1:T(8,128)}, s32[512]{0:T(512)S(1)}, s32[1,128]{1,0:T(1,128)S(1)}, bf16[2048,288]{0,1:T(8,128)(2,1)}, bf16[128,16,288]{0,2,1:T(8,128)(2,1)}, /*index=5*/f32[1,128,16]{1,2,0:T(8,128)S(1)}, ...), branch_computations={%region_12.13_spmd, %region_13.14_spmd} | conditional | flops 2898755584 | bytes 41445960 | solution.py:72
  96.0 2.5 copy.38
  98.6 2.7 fusion.68
  101.3 3.1 multiply_convert_fusion.3
  105.4 2.9 fusion.60
  108.4 2.7 fusion.66
  111.2 1.9 convolution_bitcast_fusion.4
  113.1 2.0 copy.47
  115.1 74.8 %reduce-scatter.5.cloned.1.call-done = f32[128,288]{0,1:T(8,128)} async-done(((f32[2048,288]{0,1:T(8,128)}), f32[128,288]{0,1:T(8,128)}) %reduce-scatter.5.cloned.1.call-update) | async-done | bytes 147472 | tf_op jit(solution)/shard_map/reduce_scatter | solution.py:75
  189.9 339.7 %reduce-scatter.3.cloned.1.call-done = f32[4,16,128]{2,1,0:T(8,128)} async-done(((f32[256,16,128]{2,1,0:T(8,128)}), f32[4,16,128]{2,1,0:T(8,128)}) %reduce-scatter.3.cloned.1.call-update) | async-done | bytes 32784 | tf_op jit(solution)/shard_map/reduce_scatter | solution.py:77
  529.6 86.6 %all-reduce.7.cloned.1.call-done = f32[128,288]{0,1:T(8,128)} async-done(((f32[128,288]{0,1:T(8,128)}), f32[128,288]{0,1:T(8,128)}) %all-reduce.7.cloned.1.call-update) | async-done | bytes 147472 | tf_op jit(solution)/shard_map/psum | solution.py:74
  616.2 1.6 copy.77
  (59 shorter events, 11.6 us)
Async XLA Ops:
  7.2 29.8 %copy-start = (bf16[16,256,128]{2,1,0:T(8,128)(2,1)S(1)}, bf16[16,256,128]{2,1,0:T(8,128)(2,1)}, u32[]{:S(2)}) copy-start(bf16[16,256,128]{2,1,0:T(8,128)(2,1)} %param.21) | copy-start | bytes 3145732
  7.2 54.7 %all-gather.4.cloned.1.call-start = ((), (), s32[]{:S(2)}) async-start(), calls=%async_computation.3 | async-start | bytes 1253376 | tf_op jit(solution)/shard_map/all_gather | solution.py:34
  7.9 182.0 %reduce-scatter.5.cloned.1.call-start = ((), (), s32[]{:S(2)}) async-start(), calls=%async_computation.4 | async-start | bytes 2506752 | tf_op jit(solution)/shard_map/reduce_scatter | solution.py:75
  34.1 5.6 copy-start.9
  36.9 27.0 %copy-start.1 = (bf16[1,128,16,288]{1,3,2,0:T(8,128)(2,1)S(1)}, bf16[1,128,16,288]{1,3,2,0:T(8,128)(2,1)}, u32[]{:S(2)}) copy-start(bf16[1,128,16,288]{1,3,2,0:T(8,128)(2,1)} %param.15) | copy-start | bytes 3538948
  36.9 27.0 %copy-start.16 = (s32[1,128]{1,0:T(1,128)S(1)}, s32[1,128]{1,0:T(1,128)}, u32[]{:S(2)}) copy-start(s32[1,128]{1,0:T(1,128)} %param.17) | copy-start | bytes 1540
  36.9 27.0 %copy-start.17 = (f32[1,128,16]{1,2,0:T(8,128)S(1)}, f32[1,128,16]{1,2,0:T(8,128)}, u32[]{:S(2)}) copy-start(f32[1,128,16]{1,2,0:T(8,128)} %param.18) | copy-start | bytes 24580
  63.9 1.6 copy-start.7
  64.3 1.3 copy-start.10
  68.8 1.0 copy-start.8
  74.3 2.7 copy-start.11
  77.0 1.1 copy-start.14
  78.0 2.2 copy-start.2
  80.2 2.7 copy-start.6
  86.2 2.7 copy-start.12
  88.9 1.1 copy-start.15
  89.9 2.2 copy-start.3
  92.1 2.7 copy-start.5
  98.6 2.7 copy-start.13
  105.4 3.0 copy-start.4
  111.1 418.5 %reduce-scatter.3.cloned.1.call-start = ((), (), s32[]{:S(2)}) async-start(), calls=%async_computation.2 | async-start | bytes 2129920 | tf_op jit(solution)/shard_map/reduce_scatter | solution.py:77
  115.1 501.1 %all-reduce.7.cloned.1.call-start = ((), (), s32[]{:S(2)}) async-start(), calls=%async_computation.5 | async-start | bytes 294912 | tf_op jit(solution)/shard_map/psum | solution.py:74
Sparse Core Ops, SparseCore 0:
  10.4 51.3 all-gather.3
  111.3 78.6 reduce-scatter.4
  193.0 336.6 reduce-scatter.2
  532.3 83.8 all-reduce.6
where the time goes:
time: 625 us; the launch traced here: 624 us
  waiting for transfers between devices  524 us (84%)
  matrix products  42.5 us (7%)
  between operations  19.1 us (3%)
  local copies, waits for them, and re-layouts  18.4 us (3%)
  blocking collectives  17.2 us (3%)
    reduce_scatter x1, waiting for transfers between devices, body(): lax.psum_scatter(jnp.einsum('thl,thv->lhv', saved_part, out_grad[0], pref...  340 us
    psum x1, waiting for transfers between devices, body(): summed = lax.psum(key_acc, 'head')  86.6 us
    reduce_scatter x1, waiting for transfers between devices, body(): own_rows = lax.psum_scatter(summed, 'ctx', scatter_dimension=0, tiled=True)  74.8 us
    all_gather x1, waiting for transfers between devices, body(): keys_in = lax.all_gather(latents[0], 'ctx', axis=0, tiled=True)  22.2 us
    all_gather x1, blocking collectives, body(): pos_in = lax.all_gather(positions[0], 'ctx', axis=0, tiled=True)  17.2 us
  transfers between devices with their start and end apart: 4, of which 4 were waited for; matrix products, arithmetic and copies ran while one was open for 2% of the time, Pallas kernels for 0%

commit v1 on v0

v1 whole, which is shorter than its diff:
```python
import functools

import jax
import jax.numpy as jnp
from jax import lax
from jax.experimental import pallas as pl
from jax.experimental.pallas import tpu as pltpu
from jax.sharding import PartitionSpec as P

ROPE = 32
VHEAD = 128
LATENT = 256
FULL = LATENT + ROPE
TOK = 128
EXTRA = 16
SCALING = (VHEAD + ROPE) ** -0.5
LOG2E = 1.4426950408889634
FAR = 1e30
F32 = jnp.float32
BF16 = jnp.bfloat16
NT = (((1,), (1,)), ((), ()))
VM = pl.BlockSpec(memory_space=pltpu.VMEM)
PARAMS = pltpu.CompilerParams(vmem_limit_bytes=48 << 20)


def dot(a, b):
    return jnp.dot(a, b, preferred_element_type=F32)


def dot_nt(a, b):
    return lax.dot_general(a, b, NT, preferred_element_type=F32)


def both(ref, pair):
    return jnp.concatenate([ref[2 * pair], ref[2 * pair + 1]], axis=1)


def both_rows(ref, pair):
    return jnp.concatenate([ref[pl.ds(2 * pair, 1), :], ref[pl.ds(2 * pair + 1, 1), :]], axis=1)


def call(kernel, outs, scratch=(), flops=0, nbytes=4 << 20, exps=0):
    return pl.pallas_call(
        kernel,
        out_shape=outs,
        scratch_shapes=list(scratch),
        compiler_params=PARAMS,
        cost_estimate=pl.CostEstimate(flops=flops, bytes_accessed=nbytes, transcendentals=exps),
    )


def shape(dims, dtype):
    return jax.ShapeDtypeStruct(dims, dtype)


def payload_kernel(lat_ref, pos_ref, out_ref):
    pos = pos_ref[...].astype(F32)
    base = jnp.min(pos, axis=1, keepdims=True)
    rank = jnp.broadcast_to(base * (1.0 / TOK), (1, TOK))
    extra = jnp.concatenate([rank, pos - base, jnp.zeros((EXTRA - 2, TOK), F32)], axis=0).astype(BF16)
    for j in range(out_ref.shape[0]):
        out_ref[j, :FULL] = lat_ref[...]
        out_ref[j, FULL:] = extra


def prologue_kernel(
    out_grad, saved, value_up, queries, lat_ref, pos_ref, lse, lat_grad, lat_scaled, delta, weight_part, key_own, dl_own,
    grad_s, saved_s, part_s, key_s,
):
    heads = queries.shape[0]
    groups = part_s.shape[0]
    grad_s[...] = out_grad[...].astype(F32)
    saved_s[0] = saved[:, :VHEAD].astype(F32)
    saved_s[1] = saved[:, VHEAD:].astype(F32)
    width = LATENT // groups

    def one(h, _):
        grad_h = grad_s[pl.ds(h, TOK, stride=heads), :].astype(BF16)
        saved_h = jnp.concatenate([saved_s[c, pl.ds(h, TOK, stride=heads), :].T for c in range(2)], axis=0)
        lat = dot_nt(value_up[h], grad_h)
        scaled = (lat * SCALING).astype(BF16)
        lat_grad[h] = lat.astype(BF16)
        lat_scaled[h] = scaled
        delta[pl.ds(h, 1), :] = jnp.sum(scaled.astype(F32) * saved_h, axis=0, keepdims=True)
        part = dot(saved_h.astype(BF16), grad_h)
        part_s[:, pl.ds(width * h, width), :] = part.reshape(groups, width, VHEAD)
        return 0

    lax.fori_loop(0, heads, one, 0)
    weight_part[...] = part_s[...].astype(BF16)

    key_s[...] = lat_ref[...].T
    pos_q = pos_ref[...].astype(F32)
    pos_k = jnp.broadcast_to(pos_q, (TOK, TOK)).T
    visible = pos_k <= jnp.broadcast_to(pos_q, (TOK, TOK))
    visible = jnp.concatenate([visible, visible], axis=1)
    key_own[...] = jnp.zeros_like(key_own)
    for pair in range(heads // 2):
        q2 = both(queries, pair)
        logits = dot(key_s[...], q2)
        weights = jnp.where(visible, jnp.exp2(logits * (SCALING * LOG2E) - both_rows(lse, pair) * LOG2E), 0.0)
        dot_value = dot(key_s[:, :LATENT], both(lat_scaled, pair))
        dl = (weights * (dot_value - both_rows(delta, pair))).astype(BF16)
        dl_own[:, 256 * pair : 256 * pair + 256] = dl
        key_own[...] += dot_nt(q2, dl)
        key_own[:LATENT] += dot_nt(both(lat_grad, pair), weights.astype(BF16))


def attention_kernel(chunk_blocks, recv, own, queries, lat_grad, lat_scaled, delta, lse, dl_own, own_index, key_acc, dl_all, keys_t, key_s):
    blocks = recv.shape[0]
    heads = queries.shape[0]
    rank_q = own[0, FULL : FULL + 1, :].astype(F32)
    for j in range(blocks):
        keys_t[:, TOK * j : TOK * j + TOK] = recv[j, :FULL]
        key_s[TOK * j : TOK * j + TOK, :] = recv[j, :FULL].T
    key_acc[...] = jnp.zeros_like(key_acc)
    rows = chunk_blocks * TOK
    for chunk in range(blocks // chunk_blocks):
        lo, hi = chunk * rows, chunk * rows + rows
        far = [
            jnp.where(recv[chunk * chunk_blocks + j, FULL : FULL + 1, :].astype(F32) < rank_q, 0.0, FAR)
            for j in range(chunk_blocks)
        ]
        far = [jnp.concatenate([f, f], axis=1) for f in far]

        def one(pair, _):
            q2 = both(queries, pair)
            logits = dot(key_s[lo:hi, :], q2)
            dot_value = dot(key_s[lo:hi, :LATENT], both(lat_scaled, pair))
            lse2 = both_rows(lse, pair) * LOG2E
            delta2 = both_rows(delta, pair)
            weights = jnp.concatenate(
                [
                    jnp.exp2(logits[TOK * j : TOK * j + TOK] * (SCALING * LOG2E) - (lse2 + far[j]))
                    for j in range(chunk_blocks)
                ],
                axis=0,
            )
            dl = (weights * (dot_value - delta2)).astype(BF16)
            dl_all[pair, lo:hi, :] = dl
            lat2 = both(lat_grad, pair)
            key_acc[:LATENT, lo:hi] += dot_nt(
                jnp.concatenate([q2[:LATENT], lat2], axis=1),
                jnp.concatenate([dl, weights.astype(BF16)], axis=1),
            )
            key_acc[LATENT:, lo:hi] += dot_nt(q2[LATENT:], dl)
            return 0

        lax.fori_loop(0, heads // 2, one, 0, unroll=2)
    at = pl.multiple_of(own_index[0] * TOK, TOK)
    for pair in range(heads // 2):
        dl_all[pair, pl.ds(at, TOK), :] = dl_own[:, 256 * pair : 256 * pair + 256]


def pack_kernel(key_acc, key_own, recv, own, weight_recv, out_ref):
    rank_q = own[0, FULL : FULL + 1, :].astype(F32)
    rows = out_ref.shape[1] - FULL
    for j in range(out_ref.shape[0]):
        mine = jnp.where(recv[j, FULL : FULL + 1, :].astype(F32) == rank_q, 1.0, 0.0)
        out_ref[j, :FULL] = (key_acc[:, TOK * j : TOK * j + TOK] + mine * key_own[...]).astype(BF16)
        total = weight_recv[0, rows * j : rows * j + rows].astype(F32)
        for d in range(1, weight_recv.shape[0]):
            total = total + weight_recv[d, rows * j : rows * j + rows].astype(F32)
        out_ref[j, FULL:] = total.astype(BF16)


def query_kernel(keys_t, dl_all, out_ref):
    def one(pair, _):
        grad = dot(keys_t[...], dl_all[pair]).astype(BF16)
        out_ref[2 * pair] = grad[:, :TOK]
        out_ref[2 * pair + 1] = grad[:, TOK:]
        return 0

    lax.fori_loop(0, dl_all.shape[0], one, 0)


def sum_kernel(recv, key_ref, weight_ref, part_s):
    total = recv[0].astype(F32)
    for j in range(1, recv.shape[0]):
        total = total + recv[j].astype(F32)
    key_ref[...] = total[:FULL].astype(BF16)
    part_s[...] = total[FULL:]
    width, heads = weight_ref.shape[0], weight_ref.shape[1]
    for i in range(width):
        weight_ref[i] = part_s[pl.ds(i, heads, stride=width), :]


def body(queries, latents, positions, lse, saved_out, out_grad, value_up):
    n_dp, n_ctx = lax.axis_size("dp"), lax.axis_size("ctx")
    heads = queries.shape[2]
    groups = n_dp * n_ctx
    width = LATENT // groups
    slab = n_ctx * TOK
    pairs = heads // 2
    q_t = jnp.transpose(queries[0], (1, 2, 0))
    lat_t = latents[0].T
    lse_t = lse[0].T
    payload = call(payload_kernel, shape((n_ctx, FULL + EXTRA, TOK), BF16))(lat_t, positions)
    recv = lax.all_to_all(payload, "ctx", 0, 0)

    lat_grad, lat_scaled, delta, weight_part, key_own, dl_own = call(
        prologue_kernel,
        [
            shape((heads, LATENT, TOK), BF16),
            shape((heads, LATENT, TOK), BF16),
            shape((heads, TOK), F32),
            shape((groups, heads * width, VHEAD), BF16),
            shape((FULL, TOK), F32),
            shape((TOK, heads * TOK), BF16),
        ],
        [
            pltpu.VMEM((TOK * heads, VHEAD), F32),
            pltpu.VMEM((2, TOK * heads, VHEAD), F32),
            pltpu.VMEM((groups, heads * width, VHEAD), F32),
            pltpu.VMEM((TOK, FULL), BF16),
        ],
        flops=2 * heads * TOK * TOK * (1400 + 512),
        nbytes=8 << 20,
        exps=heads * TOK * TOK,
    )(
        out_grad[0].reshape(TOK * heads, VHEAD),
        saved_out[0].reshape(TOK * heads, LATENT),
        value_up,
        q_t,
        lat_t,
        positions,
        lse_t,
    )
    weight_recv = lax.all_to_all(weight_part.reshape(n_dp, n_ctx * heads * width, VHEAD), "dp", 0, 0)

    own_index = lax.axis_index("ctx").astype(jnp.int32).reshape(1)
    key_acc, dl_all, keys_t = pl.pallas_call(
        functools.partial(attention_kernel, 4),
        out_shape=[
            shape((FULL, slab), F32),
            shape((pairs, slab, 256), BF16),
            shape((FULL, slab), BF16),
        ],
        in_specs=[VM] * 8 + [pl.BlockSpec(memory_space=pltpu.SMEM)],
        out_specs=[VM] * 3,
        scratch_shapes=[pltpu.VMEM((slab, FULL), BF16)],
        compiler_params=PARAMS,
        cost_estimate=pl.CostEstimate(
            flops=2 * slab * heads * TOK * 1100, bytes_accessed=16 << 20, transcendentals=slab * heads * TOK
        ),
    )(recv, payload[:1], q_t, lat_grad, lat_scaled, delta, lse_t, dl_own, own_index)

    packed = call(pack_kernel, shape((n_ctx, FULL + heads * width, TOK), BF16))(
        key_acc, key_own, recv, payload[:1], weight_recv
    )
    summed = lax.all_to_all(packed, "ctx", 0, 0)
    query_grad = call(
        query_kernel, shape((heads, FULL, TOK), BF16), flops=2 * slab * heads * TOK * FULL, nbytes=12 << 20
    )(keys_t, dl_all)
    key_part, weight_share = call(
        sum_kernel,
        [shape((FULL, TOK), BF16), shape((width, heads, VHEAD), F32)],
        [pltpu.VMEM((heads * width, VHEAD), F32)],
    )(summed)
    key_parts = lax.all_gather(key_part, "head")
    key_grad = jnp.sum(key_parts.astype(F32), axis=0)
    return (jnp.transpose(query_grad, (2, 0, 1))[None], key_grad.T[None], weight_share)


def solution(mesh):
    return jax.shard_map(
        body,
        mesh=mesh,
        in_specs=(
            P("dp", "ctx", "head", None),
            P("dp", "ctx", None),
            P("dp", "ctx"),
            P("dp", "ctx", "head"),
            P("dp", "ctx", "head", None),
            P("dp", "ctx", "head", None),
            P("head", None, None),
        ),
        out_specs=(
            P("dp", "ctx", "head", None),
            P("dp", "ctx", None),
            P(("dp", "ctx"), "head", None),
        ),
        check_vma=False,
    )
```

time: 625 us -> 109 us (0.17)
  waiting for transfers between devices: 524 us -> 13.6 us
  Pallas kernels: 0 us -> 47.2 us
  matrix products: 42.5 us -> 0 us
  starting transfers between devices: 0.16 us -> 20.4 us
  between operations: 19.1 us -> 0.76 us
  blocking collectives: 17.2 us -> 10.4 us
    reduce_scatter x2 -> x0, waiting for transfers between devices: 414 us -> none  [the longest x1 340 us: body(): lax.psum_scatter(jnp.einsum('thl,thv->lhv', saved_part, out_grad[0], pref...]
    psum x1 -> x0, waiting for transfers between devices: 86.6 us -> none  [body(): summed = lax.psum(key_acc, 'head')]
    pallas_call x0 -> x6, Pallas kernels: none -> 47.2 us  [the longest x1 25.3 us: body(): pl.pallas_call(functools.partial(attention_kernel, 4), out_shape=[shape((...]
    dot_general x22 -> x0, matrix products: 42.5 us -> none  [the longest x4 9.56 us: update(): jnp.einsum('thl,kl->thk', lat_grad, key_rows[:, :latent_width], preferred...]
    all_gather x1 -> x0, waiting for transfers between devices: 22.2 us -> none  [body(): keys_in = lax.all_gather(latents[0], 'ctx', axis=0, tiled=True)]
    all_to_all x0 -> x3, starting transfers between devices: none -> 20.4 us  [the longest x1 8.18 us: body(): lax.all_to_all(weight_part.reshape(n_dp, n_ctx * heads * width, VHEAD), '...]
    all_to_all x0 -> x3, waiting for transfers between devices: none -> 13.6 us  [the longest x1 9.65 us: body(): summed = lax.all_to_all(packed, 'ctx', 0, 0)]
    unnamed x12 -> x48, local copies, waits for them, and re-layouts: 4.46 us -> 14.7 us
  transfers between devices with their start and end apart: 4 -> 3, of which waited for: 4 -> 2; matrix products, arithmetic and copies ran while one was open for 2% -> 1% of each run, Pallas kernels for 0% -> 39%
where the time goes in v1:
time: 109 us
  Pallas kernels  47.2 us (43%)
  starting transfers between devices  20.4 us (19%)
  local copies, waits for them, and re-layouts  15.6 us (14%)
  waiting for transfers between devices  13.6 us (12%)
  blocking collectives  10.4 us (10%)
    pallas_call x1, Pallas kernels, body(): pl.pallas_call(functools.partial(attention_kernel, 4), out_shape=[shape((...  25.3 us
    unnamed x48, local copies, waits for them, and re-layouts  14.7 us
    all_gather x1, blocking collectives, body(): key_parts = lax.all_gather(key_part, 'head')  10.4 us
    all_to_all x1, waiting for transfers between devices, body(): summed = lax.all_to_all(packed, 'ctx', 0, 0)  9.65 us
    pallas_call x1, Pallas kernels, body(): call(prologue_kernel, [shape((heads, LATENT, TOK), BF16), shape((heads, L...  8.41 us
    pallas_call x1, Pallas kernels, body(): call(query_kernel, shape((heads, FULL, TOK), BF16), flops=2 * slab * head...  8.27 us
    all_to_all x1, starting transfers between devices, body(): lax.all_to_all(weight_part.reshape(n_dp, n_ctx * heads * width, VHEAD), '...  8.18 us
    all_to_all x1, starting transfers between devices, body(): recv = lax.all_to_all(payload, 'ctx', 0, 0)  7.73 us
  transfers between devices with their start and end apart: 3, of which 2 were waited for; matrix products, arithmetic and copies ran while one was open for 1% of the time, Pallas kernels for 39%

profile of v1, /device:TPU:1, one launch (start us, length us, event | category | flops | bytes accessed | tf_op | source)
XLA Modules:
  0.0 108.6 jit_solution(3657315406775241279)
XLA Ops:
  0.6 0.0 copy-start.8
  0.6 0.9 copy-done.8
  1.5 0.7 copy-done.14
  2.2 1.2 %shard_map.94 = bf16[16,304,128]{2,1,0:T(8,128)(2,1)} custom-call(bf16[288,128]{1,0:T(8,128)(2,1)S(1)} %bitcast.26, s32[1,128]{1,0:T(1,128)S(1)} %copy-done.14), custom_call_target="tpu_custom_call" | custom-call | bytes 4194304 | tf_op jit(solution)/shard_map/pallas_call | solution.py:198
  3.4 0.0 copy-start.15
  3.4 7.7 %all-to-all-start = ((bf16[16,304,128]{2,1,0:T(8,128)(2,1)}), bf16[16,304,128]{2,1,0:T(8,128)(2,1)S(1)}, u32[]{:S(2)}, u32[]{:S(2)}) async-start(bf16[16,304,128]{2,1,0:T(8,128)(2,1)} %shard_map.94), calls=%async_computation | async-start | bytes 2490368 | tf_op jit(solution)/shard_map/all_to_all | solution.py:199
  11.2 8.4 %shard_map.95 = (bf16[16,256,128]{2,1,0:T(8,128)(2,1)S(1)}, bf16[16,256,128]{2,1,0:T(8,128)(2,1)S(1)}, f32[16,128]{1,0:T(8,128)S(1)}, bf16[64,64,128]{2,1,0:T(8,...) custom-call(bf16[2048,128]{1,0:T(8,128)(2,1)S(1)} %bitcast.25, bf16[2048,256]{1,0:T(8,128)(2,1)S(1)} %bitcast.24, ...), custom_call_target="tpu_custom_call" | custom-call | flops 1002438656 | bytes 8388608 | tf_op jit(solution)/shard_map/pallas_call | solution.py:201
  19.6 1.0 copy-done.5
  20.6 0.7 copy-done.10
  21.3 1.0 copy-done.16
  22.3 1.0 copy-done.18
  23.3 0.8 copy-done.20
  24.1 0.6 copy-done.22
  24.7 3.9 %all-to-all-done.recv = bf16[16,304,128]{2,1,0:T(8,128)(2,1)S(1)} async-done(((bf16[16,304,128]{2,1,0:T(8,128)(2,1)}), bf16[16,304,128]{2,1,0:T(8,128)(2,1)S(1)}, u32[]{:S(2)}, u32[]{:S(2)}) %all-to-all-start) | async-done | bytes 1245216 | tf_op jit(solution)/shard_map/all_to_all | solution.py:199
  28.6 8.2 %all-to-all-start.1 = ((bf16[4,1024,128]{2,1,0:T(8,128)(2,1)}), bf16[4,1024,128]{2,1,0:T(8,128)(2,1)S(1)}, u32[]{:S(2)}, u32[]{:S(2)}) async-start(bf16[4,1024,128]{2,1,0:T(8,128)(2,1)} %bitcast.23), calls=%async_computation.1 | async-start | bytes 2097152 | tf_op jit(solution)/shard_map/all_to_all | solution.py:229
  36.8 0.9 slice.5.own
  37.7 0.7 copy-done.13
  38.4 1.2 %copy-done.17 = bf16[16,256,128]{2,1,0:T(8,128)(2,1)S(1)} copy-done((bf16[16,256,128]{2,1,0:T(8,128)(2,1)S(1)}, bf16[16,256,128]{2,1,0:T(8,128)(2,1)}, u32[]{:S(2)}) %copy-start.17) | copy-done | bytes 1048600
  39.6 1.2 %copy-done.19 = bf16[16,256,128]{2,1,0:T(8,128)(2,1)S(1)} copy-done((bf16[16,256,128]{2,1,0:T(8,128)(2,1)S(1)}, bf16[16,256,128]{2,1,0:T(8,128)(2,1)}, u32[]{:S(2)}) %copy-start.19) | copy-done | bytes 1048600
  40.8 1.0 copy-done.21
  41.9 0.7 copy-done.23
  42.6 25.3 %shard_map.96 = (f32[288,2048]{1,0:T(8,128)}, bf16[8,2048,256]{2,1,0:T(8,128)(2,1)}, bf16[288,2048]{1,0:T(8,128)(2,1)S(1)}) custom-call(bf16[16,304,128]{2,1,0:T(8,128)(2,1)} %copy-done, bf16[1,304,128]{2,1,0:T(8,128)(2,1)S(1)} %slice.5.own, bf16[16,288,128]{2,1,0:T(8,128)(2,1)S(1)} %bitcast.22, bf16[16,256,128]{2,1,0:T(8,128)(2,1)S(1)} %copy-done.17, ...), custom_call_target="tpu_custom_call" | custom-call | flops 9227468800 | bytes 16777216 | tf_op jit(solution)/shard_map/pallas_call | solution.py:232
  67.8 1.0 copy-done.3
  68.8 1.3 %copy-done.1 = bf16[16,304,128]{2,1,0:T(8,128)(2,1)S(1)} copy-done((bf16[16,304,128]{2,1,0:T(8,128)(2,1)S(1)}, bf16[16,304,128]{2,1,0:T(8,128)(2,1)}, u32[]{:S(2)}) %copy-start.1) | copy-done | bytes 1245208
  70.1 0.9 copy-done.11
  71.0 3.2 %shard_map.98 = bf16[16,352,128]{2,1,0:T(8,128)(2,1)} custom-call(f32[288,2048]{1,0:T(8,128)} %get-tuple-element.20.key_acc, f32[288,128]{1,0:T(8,128)S(1)} %copy-done.11, bf16[16,304,128]{2,1,0:T(8,128)(2,1)S(1)} %copy-done.1, bf16[1,304,128]{2,1,0:T(8,128)(2,1)S(1)} %slice.5.own, bf16[4,1024,128]{2,1,0:T(8,128)(2,1)S(1)} %all-to-all-done.1.weight_recv), custom_call_target="tpu_custom_call" | custom-call | bytes 4194304 | tf_op jit(solution)/shard_map/pallas_call | solution.py:248
  74.2 4.5 %all-to-all-start.2 = ((bf16[16,352,128]{2,1,0:T(8,128)(2,1)}), bf16[16,352,128]{2,1,0:T(8,128)(2,1)S(1)}, u32[]{:S(2)}, u32[]{:S(2)}) async-start(bf16[16,352,128]{2,1,0:T(8,128)(2,1)} %shard_map.98), calls=%async_computation.2 | async-start | bytes 2883584 | tf_op jit(solution)/shard_map/all_to_all | solution.py:251
  78.7 8.3 %shard_map.97 = bf16[16,288,128]{2,1,0:T(8,128)(2,1)} custom-call(bf16[288,2048]{1,0:T(8,128)(2,1)S(1)} %copy-done.4, bf16[8,2048,256]{2,1,0:T(8,128)(2,1)} %get-tuple-element.19.dl_all), custom_call_target="tpu_custom_call" | custom-call | flops 2415919104 | bytes 12582912 | tf_op jit(solution)/shard_map/pallas_call | solution.py:252
  87.0 9.7 %all-to-all-done.2.recv = bf16[16,352,128]{2,1,0:T(8,128)(2,1)S(1)} async-done(((bf16[16,352,128]{2,1,0:T(8,128)(2,1)}), bf16[16,352,128]{2,1,0:T(8,128)(2,1)S(1)}, u32[]{:S(2)}, u32[]{:S(2)}) %all-to-all-start.2) | async-done | bytes 1441824 | tf_op jit(solution)/shard_map/all_to_all | solution.py:251
  96.7 0.8 shard_map.99
  97.5 10.4 %all-gather = bf16[1152,128]{1,0:T(8,128)(2,1)S(1)} all-gather(bf16[288,128]{1,0:T(8,128)(2,1)S(1)} %get-tuple-element.23), channel_id=2, replica_groups=mesh['dp'=4,'ctx'=16,'head'=4] {'head'}, dimensions={0}, use_global_device_ids=true | all-gather | bytes 368640 | tf_op jit(solution)/shard_map/all_gather | solution.py:260
  107.9 0.7 convert_reduce_fusion
  (31 shorter events, 0.1 us)
Async XLA Ops:
  0.6 0.9 copy-start.8
  1.5 0.7 copy-start.14
  3.4 7.8 %copy-start.6 = (bf16[1,128,16,256]{3,2,1,0:T(8,128)(2,1)S(1)}, bf16[1,128,16,256]{3,2,1,0:T(8,128)(2,1)}, u32[]{:S(2)}) copy-start(bf16[1,128,16,256]{3,2,1,0:T(8,128)(2,1)} %param.11) | copy-start | bytes 3145732
  3.4 7.8 %copy-start.7 = (bf16[1,128,16,128]{3,2,1,0:T(8,128)(2,1)S(1)}, bf16[1,128,16,128]{3,2,1,0:T(8,128)(2,1)}, u32[]{:S(2)}) copy-start(bf16[1,128,16,128]{3,2,1,0:T(8,128)(2,1)} %param.12) | copy-start | bytes 1572868
  3.4 7.8 %copy-start.9 = (bf16[1,128,288]{1,2,0:T(8,128)(2,1)S(1)}, bf16[1,128,288]{1,2,0:T(8,128)(2,1)}, u32[]{:S(2)}) copy-start(bf16[1,128,288]{1,2,0:T(8,128)(2,1)} %param.8) | copy-start | bytes 221188
  3.4 7.8 %copy-start.12 = (f32[1,128,16]{1,2,0:T(8,128)S(1)}, f32[1,128,16]{1,2,0:T(8,128)}, u32[]{:S(2)}) copy-start(f32[1,128,16]{1,2,0:T(8,128)} %param.10) | copy-start | bytes 24580
  3.4 7.8 %copy-start.15 = (s32[1,128]{1,0:T(1,128)S(1)}, s32[1,128]{1,0:T(1,128)}, u32[]{:S(2)}) copy-start(s32[1,128]{1,0:T(1,128)} %pos_ref.3) | copy-start | bytes 1540
  3.4 25.2 %all-to-all-start = ((bf16[16,304,128]{2,1,0:T(8,128)(2,1)}), bf16[16,304,128]{2,1,0:T(8,128)(2,1)S(1)}, u32[]{:S(2)}, u32[]{:S(2)}) async-start(bf16[16,304,128]{2,1,0:T(8,128)(2,1)} %shard_map.94), calls=%async_computation | async-start | bytes 2490368 | tf_op jit(solution)/shard_map/all_to_all | solution.py:199
  19.6 1.0 copy-start.5
  20.6 0.7 copy-start.10
  21.3 1.0 copy-start.16
  22.3 1.0 copy-start.18
  23.3 0.8 copy-start.20
  24.1 0.6 copy-start.22
  24.7 13.0 %copy-start.2 = (bf16[1,128,16,288]{1,3,2,0:T(8,128)(2,1)S(1)}, bf16[1,128,16,288]{1,3,2,0:T(8,128)(2,1)}, u32[]{:S(2)}) copy-start(bf16[1,128,16,288]{1,3,2,0:T(8,128)(2,1)} %param.7) | copy-start | bytes 3538948
  28.6 9.1 %copy-start = (bf16[16,304,128]{2,1,0:T(8,128)(2,1)}, bf16[16,304,128]{2,1,0:T(8,128)(2,1)S(1)}, u32[]{:S(2)}) copy-start(bf16[16,304,128]{2,1,0:T(8,128)(2,1)S(1)} %all-to-all-done.recv) | copy-start | bytes 3735556
  28.6 40.2 %all-to-all-start.1 = ((bf16[4,1024,128]{2,1,0:T(8,128)(2,1)}), bf16[4,1024,128]{2,1,0:T(8,128)(2,1)S(1)}, u32[]{:S(2)}, u32[]{:S(2)}) async-start(bf16[4,1024,128]{2,1,0:T(8,128)(2,1)} %bitcast.23), calls=%async_computation.1 | async-start | bytes 2097152 | tf_op jit(solution)/shard_map/all_to_all | solution.py:229
  37.7 0.7 copy-start.13
  38.4 1.2 %copy-start.17 = (bf16[16,256,128]{2,1,0:T(8,128)(2,1)S(1)}, bf16[16,256,128]{2,1,0:T(8,128)(2,1)}, u32[]{:S(2)}) copy-start(bf16[16,256,128]{2,1,0:T(8,128)(2,1)} %copy-done.16) | copy-start | bytes 3145732
  39.6 1.2 %copy-start.19 = (bf16[16,256,128]{2,1,0:T(8,128)(2,1)S(1)}, bf16[16,256,128]{2,1,0:T(8,128)(2,1)}, u32[]{:S(2)}) copy-start(bf16[16,256,128]{2,1,0:T(8,128)(2,1)} %copy-done.18) | copy-start | bytes 3145732
  40.8 1.0 copy-start.21
  41.9 0.7 copy-start.23
  67.8 1.0 copy-start.3
  68.8 1.3 %copy-start.1 = (bf16[16,304,128]{2,1,0:T(8,128)(2,1)S(1)}, bf16[16,304,128]{2,1,0:T(8,128)(2,1)}, u32[]{:S(2)}) copy-start(bf16[16,304,128]{2,1,0:T(8,128)(2,1)} %copy-done) | copy-start | bytes 3735556
  70.1 0.9 copy-start.11
  74.2 4.5 %copy-start.4 = (bf16[288,2048]{1,0:T(8,128)(2,1)S(1)}, bf16[288,2048]{1,0:T(8,128)(2,1)}, u32[]{:S(2)}) copy-start(bf16[288,2048]{1,0:T(8,128)(2,1)} %copy-done.3) | copy-start | bytes 3538948
  74.2 22.4 %all-to-all-start.2 = ((bf16[16,352,128]{2,1,0:T(8,128)(2,1)}), bf16[16,352,128]{2,1,0:T(8,128)(2,1)S(1)}, u32[]{:S(2)}, u32[]{:S(2)}) async-start(bf16[16,352,128]{2,1,0:T(8,128)(2,1)} %shard_map.98), calls=%async_computation.2 | async-start | bytes 2883584 | tf_op jit(solution)/shard_map/all_to_all | solution.py:251

commit v2 on v1

v2 whole, which is shorter than its diff:
```python
import functools

import jax
import jax.numpy as jnp
from jax import lax
from jax.experimental import pallas as pl
from jax.experimental.pallas import tpu as pltpu
from jax.sharding import PartitionSpec as P

ROPE = 32
VHEAD = 128
LATENT = 256
FULL = LATENT + ROPE
TOK = 128
HALF = TOK // 2
SCALING = (VHEAD + ROPE) ** -0.5
LOG2E = 1.4426950408889634
FAR = 1e30
ROT = 2 * HALF
RANK = ROT + HALF * ROPE // TOK
BLOCK = RANK + 16
F32 = jnp.float32
BF16 = jnp.bfloat16
FLOPS = (1 << 33, 1 << 33)
NT = (((1,), (1,)), ((), ()))
VM = pl.BlockSpec(memory_space=pltpu.VMEM)
ANY = pl.BlockSpec(memory_space=pl.ANY)
SM = pl.BlockSpec(memory_space=pltpu.SMEM)


def vmem(mib):
    return pltpu.CompilerParams(vmem_limit_bytes=mib << 20)


def cost(flops, nbytes, exps=0):
    return pl.CostEstimate(flops=flops, bytes_accessed=nbytes, transcendentals=exps)


def shape(dims, dtype):
    return jax.ShapeDtypeStruct(dims, dtype)


def near_shape(dims, dtype):
    return pltpu.VMEM(dims, dtype)


def far_shape(dims, dtype):
    return pltpu.HBM(dims, dtype)


def held(x):
    return pltpu.with_memory_space_constraint(x, pltpu.VMEM)


def far_away(x):
    return pltpu.with_memory_space_constraint(x, pltpu.HBM)


def dot(a, b):
    return jnp.dot(a, b, preferred_element_type=F32)


def dot_nt(a, b):
    return lax.dot_general(a, b, NT, preferred_element_type=F32)


def both(ref, pair):
    return jnp.concatenate([ref[2 * pair], ref[2 * pair + 1]], axis=1)


def both_rows(ref, pair):
    return jnp.concatenate([ref[pl.ds(2 * pair, 1), :], ref[pl.ds(2 * pair + 1, 1), :]], axis=1)


def payload_kernel(lat_hbm, pos_hbm, out_hbm, block, lat_s, key_s, pos_s, in_sem, out_sem):
    lat_in = pltpu.make_async_copy(lat_hbm, lat_s, in_sem.at[0])
    pos_in = pltpu.make_async_copy(pos_hbm, pos_s, in_sem.at[1])
    lat_in.start()
    pos_in.start()
    pos_in.wait()
    base = jnp.min(pos_s[...].astype(F32), axis=1, keepdims=True)
    block[RANK:] = jnp.broadcast_to(base * (1.0 / TOK), (BLOCK - RANK, TOK)).astype(BF16)
    lat_in.wait()
    key_s[...] = lat_s[...].T
    half = key_s[pl.ds(pl.multiple_of(lax.rem(lax.axis_index("head"), 2) * HALF, HALF), HALF), :]
    block[:HALF] = half[:, :TOK]
    block[HALF:ROT] = half[:, TOK:LATENT]
    rot = half[:, LATENT:].astype(F32)
    block[ROT:RANK] = jnp.concatenate([rot[16 * g : 16 * g + 16] for g in range(HALF // 16)], axis=1).astype(BF16)
    copies = [pltpu.make_async_copy(block, out_hbm.at[j], out_sem.at[j]) for j in range(out_hbm.shape[0])]
    for copy in copies:
        copy.start()
    for copy in copies:
        copy.wait()


def prologue_kernel(out_grad_hbm, saved_hbm, up_hbm, q_hbm, lat_hbm, pos_hbm, lse_hbm, *rest):
    start, lat_hbm_out, scaled_hbm, delta_hbm, own_hbm, query_hbm, parts_hbm = rest[:7]
    queries, lse, lat_grad, lat_scaled, delta = rest[7:12]
    out_grad, saved, value_up, lat_ref, pos_ref, grad_s, saved_s, part_s, parts, key_s = rest[-15:-5]
    key_own, own_s, query_own, sem, out_sem = rest[-5:]
    core = lax.rem(lax.axis_index("head"), 2)
    moves = [
        (out_grad_hbm, out_grad),
        (saved_hbm, saved),
        (up_hbm, value_up),
        (q_hbm, queries),
        (lat_hbm, lat_ref),
        (pos_hbm, pos_ref),
        (lse_hbm, lse),
    ]
    copies = [pltpu.make_async_copy(src, dst, sem.at[i]) for i, (src, dst) in enumerate(moves)]
    for copy in copies:
        copy.start()
    heads = queries.shape[0]
    n_ctx, n_dp = part_s.shape[:2]
    width = LATENT // (n_ctx * n_dp)
    copies[0].wait()
    grad_s[...] = out_grad[...].astype(F32)
    copies[1].wait()
    saved_s[0] = saved[:, :VHEAD].astype(F32)
    saved_s[1] = saved[:, VHEAD:].astype(F32)
    for copy in copies[2:]:
        copy.wait()

    def one(h, _):
        grad_h = grad_s[pl.ds(h, TOK, stride=heads), :].astype(BF16)
        saved_h = jnp.concatenate([saved_s[c, pl.ds(h, TOK, stride=heads), :].T for c in range(2)], axis=0)
        lat = dot_nt(value_up[h], grad_h)
        scaled = (lat * SCALING).astype(BF16)
        lat_grad[h] = lat.astype(BF16)
        lat_scaled[h] = scaled
        delta[pl.ds(h, 1), :] = jnp.sum(scaled.astype(F32) * saved_h, axis=0, keepdims=True)
        part = dot(saved_h.astype(BF16), grad_h)
        for d in range(n_dp):
            rows = part[d * n_ctx * width : (d + 1) * n_ctx * width]
            part_s[:, d, pl.ds(width * h, width), :] = rows.reshape(n_ctx, width, VHEAD)
        return 0

    lax.fori_loop(0, heads, one, 0, unroll=4)
    start[...] = jnp.zeros_like(start)
    outs = [
        (parts, parts_hbm),
        (lat_grad, lat_hbm_out),
        (lat_scaled, scaled_hbm),
        (delta, delta_hbm),
        (own_s, own_hbm),
        (query_own, query_hbm),
    ]
    outs = [pltpu.make_async_copy(src, dst, out_sem.at[i]) for i, (src, dst) in enumerate(outs)]
    parts[...] = part_s[...].astype(BF16)
    for copy in outs[:4]:
        copy.start()

    key_s[...] = lat_ref[...].T
    pos_q = pos_ref[...].astype(F32)
    pos_k = jnp.broadcast_to(pos_q, (TOK, TOK)).T
    visible = pos_k <= jnp.broadcast_to(pos_q, (TOK, TOK))
    visible = jnp.concatenate([visible, visible], axis=1)
    key_own[...] = jnp.zeros_like(key_own)
    for pair in range(heads // 2):
        q2 = both(queries, pair)
        logits = dot(key_s[...], q2)
        weights = jnp.where(visible, jnp.exp2(logits * (SCALING * LOG2E) - both_rows(lse, pair) * LOG2E), 0.0)
        dot_value = dot(key_s[:, :LATENT], both(lat_scaled, pair))
        dl = (weights * (dot_value - both_rows(delta, pair))).astype(BF16)
        query_own[pair] = dot(lat_ref[...], dl)
        key_own[...] += dot_nt(q2, dl)
        key_own[:LATENT] += dot_nt(both(lat_grad, pair), weights.astype(BF16))
    own = key_own[...]
    own_s[...] = jnp.where(core == 0, own, jnp.concatenate([own[:, HALF:], own[:, :HALF]], axis=1))
    for copy in outs[4:]:
        copy.start()
    for copy in outs:
        copy.wait()


def attention_kernel(
    recv_hbm, q_hbm, lse_hbm, lat_hbm, scaled_hbm, delta_hbm, after, query_hbm, key_acc, done,
    recv, queries, lse, lat_grad, lat_scaled, delta, key_s, keys_t, query_s, sem, in_sem,
):
    heads = queries.shape[0]
    count = key_s.shape[0] // HALF
    quarter = count // 4
    moves = [(recv_hbm.at[i * quarter : (i + 1) * quarter], recv.at[i * quarter : (i + 1) * quarter]) for i in range(4)]
    moves += [(lse_hbm, lse), (delta_hbm, delta)]
    near = heads // 2
    for lo in (0, near):
        pieces = ((q_hbm, queries), (scaled_hbm, lat_scaled), (lat_hbm, lat_grad))
        moves += [(src.at[lo : lo + near], dst.at[lo : lo + near]) for src, dst in pieces]
    copies = [pltpu.make_async_copy(src, dst, in_sem.at[i]) for i, (src, dst) in enumerate(moves)]
    for copy in copies:
        copy.start()
    own = lax.axis_index("ctx")
    key_acc[...] = jnp.zeros_like(key_acc)
    for j in range(count):
        if j % quarter == 0:
            copies[j // quarter].wait()
        lo = HALF * j
        key_s[lo : lo + HALF, :TOK] = recv[j, :HALF]
        key_s[lo : lo + HALF, TOK:LATENT] = recv[j, HALF:ROT]
        rot = recv[j, ROT:RANK].astype(F32)
        for g in range(HALF // 16):
            key_s[lo + 16 * g : lo + 16 * g + 16, LATENT:] = rot[:, ROPE * g : ROPE * g + ROPE].astype(BF16)
        if j % 2:
            keys_t[:, lo - HALF : lo + HALF] = key_s[lo - HALF : lo + HALF, :].T
    rank_q = recv[own, RANK : RANK + 1, :].astype(F32)
    far = []
    for j in range(count):
        one_far = jnp.where(recv[j, RANK : RANK + 1, :].astype(F32) < rank_q, 0.0, FAR)
        far.append(jnp.concatenate([one_far, one_far], axis=1))
    def one(pair, _):
        q2 = both(queries, pair)
        logits = dot(key_s[...], q2)
        dot_value = dot(key_s[:, :LATENT], both(lat_scaled, pair))
        lse2 = both_rows(lse, pair) * LOG2E
        delta2 = both_rows(delta, pair)
        weights = jnp.concatenate(
            [
                jnp.exp2(logits[HALF * j : HALF * j + HALF] * (SCALING * LOG2E) - (lse2 + far[j]))
                for j in range(count)
            ],
            axis=0,
        )
        dl = (weights * (dot_value - delta2)).astype(BF16)
        query_s[pair] = dot(keys_t[...], dl)
        pltpu.make_async_copy(query_s.at[pair], query_hbm.at[pair], sem.at[pair]).start()
        key_acc[:LATENT] += dot_nt(
            jnp.concatenate([q2[:LATENT], both(lat_grad, pair)], axis=1),
            jnp.concatenate([dl, weights.astype(BF16)], axis=1),
        )
        key_acc[LATENT:] += dot_nt(q2[LATENT:], dl)
        return 0

    for i in range(2):
        for copy in copies[4 + 5 * i : 9 + 3 * i]:
            copy.wait()
        lax.fori_loop(near // 2 * i, near // 2 * (i + 1), one, 0, unroll=near // 2)
    done[...] = after[: done.shape[0]]
    for pair in range(heads // 2):
        pltpu.make_async_copy(query_s.at[pair], query_hbm.at[pair], sem.at[pair]).wait()


def pack_kernel(mine, other, own_ref, after, out_ref):
    del after
    own = lax.axis_index("ctx")
    for j in range(out_ref.shape[0]):
        lo = HALF * j
        total = jnp.concatenate([mine[:, lo : lo + HALF], other[:, lo : lo + HALF]], axis=1)
        total = total + jnp.where(own == j, 1.0, 0.0) * own_ref[...]
        out_ref[j] = total.astype(BF16)


def weight_kernel(recv, friend_ref, keep_ref):
    total = recv[0].astype(F32)
    for j in range(1, recv.shape[0]):
        total = total + recv[j].astype(F32)
    dp = lax.axis_index("dp")
    friend = dp + 1 - 2 * lax.rem(dp, 2)
    for ref, index in ((friend_ref, friend), (keep_ref, dp)):
        for i, part in enumerate((index, recv.shape[1] - 1 - index)):
            chosen = total[0]
            for d in range(1, recv.shape[1]):
                chosen = jnp.where(part == d, total[d], chosen)
            ref[i] = chosen.astype(BF16)


def middle_kernel(keep, recv, stay_ref, send_ref):
    total = keep[...].astype(F32) + recv[...].astype(F32)
    stay_ref[...] = total[0]
    send_ref[...] = total[1].astype(BF16)


def query_kernel(own, mine, other, out_ref):
    for i in range(own.shape[0]):
        grad = own[i] + mine[i] + other[i]
        out_ref[2 * i] = grad[:, :TOK].astype(BF16)
        out_ref[2 * i + 1] = grad[:, TOK:].astype(BF16)


def sum_kernel(recv, stay, weight_recv, key_ref, weight_ref, part_s):
    total = recv[0].astype(F32)
    for j in range(1, recv.shape[0]):
        total = total + recv[j].astype(F32)
    key_ref[...] = total.astype(BF16)
    part_s[...] = stay[...] + weight_recv[...].astype(F32)
    width, heads = weight_ref.shape[0], weight_ref.shape[1]
    for i in range(width):
        weight_ref[i] = part_s[pl.ds(i, heads, stride=width), :]


def last_kernel(parts, out_ref):
    sides = []
    for core in range(2):
        total = parts[core].astype(F32)
        for other in range(core + 2, parts.shape[0], 2):
            total = total + parts[other].astype(F32)
        sides.append(total)
    out_ref[...] = sides[0] + jnp.concatenate([sides[1][:, HALF:], sides[1][:, :HALF]], axis=1)


def body(queries, latents, positions, lse, saved_out, out_grad, value_up):
    n_dp, n_ctx, n_head = lax.axis_size("dp"), lax.axis_size("ctx"), lax.axis_size("head")
    heads = queries.shape[2]
    groups = n_dp * n_ctx
    width = LATENT // groups
    pairs = heads // 2
    q_t = far_away(jnp.transpose(queries[0], (1, 2, 0)))
    lat_t = far_away(latents[0].T)
    lse_t = far_away(lse[0].T)
    positions = far_away(positions)
    def core_swap(x):
        return lax.ppermute(x, "head", [(i, i ^ 1) for i in range(n_head)])

    payload = pl.pallas_call(
        payload_kernel,
        out_shape=shape((n_ctx, BLOCK, TOK), BF16),
        in_specs=[ANY, ANY],
        out_specs=ANY,
        scratch_shapes=[
            pltpu.VMEM((BLOCK, TOK), BF16),
            pltpu.VMEM((FULL, TOK), BF16),
            pltpu.VMEM((TOK, FULL), BF16),
            pltpu.VMEM((1, TOK), jnp.int32),
            pltpu.SemaphoreType.DMA((2,)),
            pltpu.SemaphoreType.DMA((n_ctx,)),
        ],
        compiler_params=vmem(2),
    )(lat_t, positions)
    recv_mine = lax.all_to_all(payload, "ctx", 0, 0)

    part_rows = heads * width
    start, lat_grad, lat_scaled, delta, key_own, query_own, parts = pl.pallas_call(
        prologue_kernel,
        out_shape=[
            near_shape((8, TOK), F32),
            far_shape((heads, LATENT, TOK), BF16),
            far_shape((heads, LATENT, TOK), BF16),
            far_shape((heads, TOK), F32),
            far_shape((FULL, TOK), F32),
            far_shape((pairs, FULL, 2 * TOK), F32),
            far_shape((n_ctx, n_dp, part_rows, VHEAD), BF16),
        ],
        in_specs=[ANY] * 7,
        out_specs=[VM] + [ANY] * 6,
        scratch_shapes=[
            pltpu.VMEM((heads, FULL, TOK), BF16),
            pltpu.VMEM((heads, TOK), F32),
            pltpu.VMEM((heads, LATENT, TOK), BF16),
            pltpu.VMEM((heads, LATENT, TOK), BF16),
            pltpu.VMEM((heads, TOK), F32),
            pltpu.VMEM((TOK * heads, VHEAD), BF16),
            pltpu.VMEM((TOK * heads, LATENT), BF16),
            pltpu.VMEM((heads, LATENT, VHEAD), BF16),
            pltpu.VMEM((FULL, TOK), BF16),
            pltpu.VMEM((1, TOK), jnp.int32),
            pltpu.VMEM((TOK * heads, VHEAD), F32),
            pltpu.VMEM((2, TOK * heads, VHEAD), F32),
            pltpu.VMEM((n_ctx, n_dp, part_rows, VHEAD), F32),
            pltpu.VMEM((n_ctx, n_dp, part_rows, VHEAD), BF16),
            pltpu.VMEM((TOK, FULL), BF16),
            pltpu.VMEM((FULL, TOK), F32),
            pltpu.VMEM((FULL, TOK), F32),
            pltpu.VMEM((pairs, FULL, 2 * TOK), F32),
            pltpu.SemaphoreType.DMA((7,)),
            pltpu.SemaphoreType.DMA((6,)),
        ],
        compiler_params=vmem(28),
        cost_estimate=cost(2 * heads * TOK * TOK * 1900, 8 << 20, heads * TOK * TOK),
    )(
        far_away(out_grad[0].reshape(TOK * heads, VHEAD)),
        far_away(saved_out[0].reshape(TOK * heads, LATENT)),
        far_away(value_up),
        q_t,
        lat_t,
        positions,
        lse_t,
    )
    recv_other = core_swap(recv_mine)

    def attend(recv, after, flops):
        rows = n_ctx * HALF
        return pl.pallas_call(
            attention_kernel,
            out_shape=[
                far_shape((pairs, FULL, 2 * TOK), F32),
                near_shape((FULL, rows), F32),
                near_shape((8, TOK), F32),
            ],
            in_specs=[ANY] * 6 + [VM],
            out_specs=[ANY, VM, VM],
            scratch_shapes=[
                pltpu.VMEM((n_ctx, BLOCK, TOK), BF16),
                pltpu.VMEM((heads, FULL, TOK), BF16),
                pltpu.VMEM((heads, TOK), F32),
                pltpu.VMEM((heads, LATENT, TOK), BF16),
                pltpu.VMEM((heads, LATENT, TOK), BF16),
                pltpu.VMEM((heads, TOK), F32),
                pltpu.VMEM((rows, FULL), BF16),
                pltpu.VMEM((FULL, rows), BF16),
                pltpu.VMEM((pairs, FULL, 2 * TOK), F32),
                pltpu.SemaphoreType.DMA((pairs,)),
                pltpu.SemaphoreType.DMA((12,)),
            ],
            compiler_params=vmem(24),
            cost_estimate=cost(flops, 1 << 16),
        )(recv, q_t, lse_t, far_away(lat_grad), far_away(lat_scaled), far_away(delta), held(after))

    query_1, sum_1, step = attend(recv_mine, start, FLOPS[0])
    query_2, sum_2, step = attend(recv_other, step, FLOPS[1])

    weight_ctx = lax.all_to_all(parts, "ctx", 0, 0)
    send_1, keep_1 = pl.pallas_call(
        weight_kernel,
        out_shape=[
            shape((2, part_rows, VHEAD), BF16),
            shape((2, part_rows, VHEAD), BF16),
        ],
        in_specs=[VM],
        out_specs=[VM] * 2,
        compiler_params=vmem(4),
        cost_estimate=cost(1 << 16, 1 << 16),
    )(weight_ctx)

    packed = pl.pallas_call(
        pack_kernel,
        out_shape=shape((n_ctx, FULL, TOK), BF16),
        in_specs=[VM] * 3 + [ANY],
        out_specs=VM,
        compiler_params=vmem(6),
    )(held(sum_1), held(sum_2), key_own, weight_ctx)
    summed = lax.all_to_all(packed, "ctx", 0, 0)

    recv_1 = lax.ppermute(send_1, "dp", [(i, i ^ 1) for i in range(n_dp)])
    stay, send_2 = pl.pallas_call(
        middle_kernel,
        out_shape=[shape((part_rows, VHEAD), F32), shape((part_rows, VHEAD), BF16)],
        in_specs=[VM] * 2,
        out_specs=[VM] * 2,
        compiler_params=vmem(2),
        cost_estimate=cost(1 << 16, 1 << 16),
    )(keep_1, recv_1)
    recv_2 = lax.ppermute(send_2, "dp", [(i, n_dp - 1 - i) for i in range(n_dp)])
    query_grad = pl.pallas_call(
        query_kernel,
        out_shape=shape((heads, FULL, TOK), BF16),
        grid=(4,),
        in_specs=[pl.BlockSpec((pairs // 4, FULL, 2 * TOK), lambda p: (p, 0, 0))] * 3,
        out_specs=pl.BlockSpec((heads // 4, FULL, TOK), lambda p: (p, 0, 0)),
        compiler_params=vmem(12),
        cost_estimate=cost(1 << 33, 12 << 20),
    )(*[far_away(x) for x in (query_own, query_1, query_2)])
    key_part, weight_share = pl.pallas_call(
        sum_kernel,
        out_shape=[shape((FULL, TOK), BF16), shape((width, heads, VHEAD), F32)],
        in_specs=[VM] * 3,
        out_specs=[VM] * 2,
        scratch_shapes=[pltpu.VMEM((heads * width, VHEAD), F32)],
        compiler_params=vmem(4),
    )(summed, stay, recv_2)
    key_grad = pl.pallas_call(
        last_kernel,
        out_shape=shape((FULL, TOK), F32),
        in_specs=[VM],
        out_specs=VM,
        compiler_params=vmem(2),
    )(lax.all_gather(key_part, "head"))
    return (jnp.transpose(query_grad, (2, 0, 1))[None], key_grad.T[None], weight_share)


def solution(mesh):
    return jax.shard_map(
        body,
        mesh=mesh,
        in_specs=(
            P("dp", "ctx", "head", None),
            P("dp", "ctx", None),
            P("dp", "ctx"),
            P("dp", "ctx", "head"),
            P("dp", "ctx", "head", None),
            P("dp", "ctx", "head", None),
            P("head", None, None),
        ),
        out_specs=(
            P("dp", "ctx", "head", None),
            P("dp", "ctx", None),
            P(("dp", "ctx"), "head", None),
        ),
        check_vma=False,
    )
```

time: 109 us -> 88.5 us (0.81)
  local copies, waits for them, and re-layouts: 15.6 us -> 0.01 us
  starting transfers between devices: 20.4 us -> 28.8 us
  waiting for transfers between devices: 13.6 us -> 7.68 us
  Pallas kernels: 47.2 us -> 42.8 us
  blocking collectives: 10.4 us -> 7.92 us
    unnamed x48 -> x2, local copies, waits for them, and re-layouts: 14.7 us -> 0.01 us
    ppermute x0 -> x3, starting transfers between devices: none -> 9.85 us  [the longest x1 5.17 us: body(): lax.ppermute(send_2, 'dp', [(i, n_dp - 1 - i) for i in range(n_dp)])]
    all_to_all x1, waiting for transfers between devices: 9.65 us -> 3.9 us  [body(): summed = lax.all_to_all(packed, 'ctx', 0, 0)]
    pallas_call x6 -> x10, Pallas kernels: 47.2 us -> 42.8 us  [the longest x2 23.3 us: attend(): pl.pallas_call(attention_kernel, out_shape=[far_shape((pairs, FULL, 2 * T...]
    all_to_all x2, starting transfers between devices: 15.9 us -> 12.1 us  [the longest x1 7.6 us: body(): recv_mine = lax.all_to_all(payload, 'ctx', 0, 0)]
    all_gather x1, blocking collectives: 10.4 us -> 7.92 us  [body(): lax.all_gather(key_part, 'head')]
    all_to_all x1, starting transfers between devices: 4.5 us -> 6.86 us  [body(): summed = lax.all_to_all(packed, 'ctx', 0, 0)]
    all_to_all x2, waiting for transfers between devices: 3.94 us -> 2.18 us  [the longest x1 2.17 us: body(): recv_mine = lax.all_to_all(payload, 'ctx', 0, 0)]
  transfers between devices with their start and end apart: 3 -> 6, of which waited for: 2 -> 3; matrix products, arithmetic and copies ran while one was open for 1% -> 0% of each run, Pallas kernels for 39% -> 43%
where the time goes in v2:
time: 88.5 us; the launch traced here: 88 us
  Pallas kernels  42.8 us (48%)
  starting transfers between devices  28.8 us (33%)
  blocking collectives  7.92 us (9%)
  waiting for transfers between devices  7.68 us (9%)
    pallas_call x2, Pallas kernels, attend(): pl.pallas_call(attention_kernel, out_shape=[far_shape((pairs, FULL, 2 * T...  23.3 us
    pallas_call x1, Pallas kernels, body(): pl.pallas_call(prologue_kernel, out_shape=[near_shape((8, TOK), F32), far...  9.42 us
    all_gather x1, blocking collectives, body(): lax.all_gather(key_part, 'head')  7.92 us
    all_to_all x1, starting transfers between devices, body(): recv_mine = lax.all_to_all(payload, 'ctx', 0, 0)  7.6 us
    all_to_all x1, starting transfers between devices, body(): summed = lax.all_to_all(packed, 'ctx', 0, 0)  6.86 us
    ppermute x1, starting transfers between devices, body(): lax.ppermute(send_2, 'dp', [(i, n_dp - 1 - i) for i in range(n_dp)])  5.17 us
    pallas_call x1, Pallas kernels, body(): pl.pallas_call(query_kernel, out_shape=shape((heads, FULL, TOK), BF16), g...  4.62 us
    all_to_all x1, starting transfers between devices, body(): weight_ctx = lax.all_to_all(parts, 'ctx', 0, 0)  4.5 us
  transfers between devices with their start and end apart: 6, of which 3 were waited for; matrix products, arithmetic and copies ran while one was open for 0% of the time, Pallas kernels for 43%

profile of v2, /device:TPU:1, one launch (start us, length us, event | category | flops | bytes accessed | tf_op | source)
XLA Modules:
  0.0 88.0 jit_solution(13357072773712132113)
XLA Ops:
  0.6 2.1 %shard_map.95 = bf16[16,160,128]{2,1,0:T(8,128)(2,1)} custom-call(bf16[288,128]{1,0:T(8,128)(2,1)} %bitcast.24, s32[1,128]{1,0:T(1,128)} %pos_hbm.3), custom_call_target="tpu_custom_call" | custom-call | tf_op jit(solution)/shard_map/pallas_call | solution.py:315
  2.7 7.6 %all-to-all-start = ((bf16[16,160,128]{2,1,0:T(8,128)(2,1)}), bf16[16,160,128]{2,1,0:T(8,128)(2,1)S(1)}, u32[]{:S(2)}, u32[]{:S(2)}) async-start(bf16[16,160,128]{2,1,0:T(8,128)(2,1)} %shard_map.95), calls=%async_computation | async-start | bytes 1310720 | tf_op jit(solution)/shard_map/all_to_all | solution.py:330
  10.3 9.4 %shard_map.94 = (f32[8,128]{1,0:T(8,128)S(1)}, bf16[16,256,128]{2,1,0:T(8,128)(2,1)}, bf16[16,256,128]{2,1,0:T(8,128)(2,1)}, f32[16,128]{1,0:T(8,128)}, f32[288,...) custom-call(bf16[2048,128]{1,0:T(8,128)(2,1)} %bitcast.23, bf16[2048,256]{1,0:T(8,128)(2,1)} %bitcast.22, ...), custom_call_target="tpu_custom_call" | custom-call | flops 996147200 | bytes 8388608 | tf_op jit(solution)/shard_map/pallas_call | solution.py:333
  19.7 2.2 %all-to-all-done.recv_hbm = bf16[16,160,128]{2,1,0:T(8,128)(2,1)S(1)} async-done(((bf16[16,160,128]{2,1,0:T(8,128)(2,1)}), bf16[16,160,128]{2,1,0:T(8,128)(2,1)S(1)}, u32[]{:S(2)}, u32[]{:S(2)}) %all-to-all-start) | async-done | bytes 655392 | tf_op jit(solution)/shard_map/all_to_all | solution.py:330
  21.9 4.5 %all-to-all-start.1 = ((bf16[16,4,64,128]{3,2,1,0:T(8,128)(2,1)}), bf16[16,4,64,128]{3,2,1,0:T(8,128)(2,1)S(1)}, u32[]{:S(2)}, u32[]{:S(2)}) async-start(bf16[16,4,64,128]{3,2,1,0:T(8,128)(2,1)} %get-tuple-element.32), calls=%async_computation.1 | async-start | bytes 2097152 | tf_op jit(solution)/shard_map/all_to_all | solution.py:412
  26.4 1.6 %collective-permute-start = (bf16[16,160,128]{2,1,0:T(8,128)(2,1)S(1)}, bf16[16,160,128]{2,1,0:T(8,128)(2,1)S(1)}, u32[]{:S(2)}, u32[]{:S(2)}) collective-permute-start(bf16[16,160,128]{2,1,0:T(8,128)(2,1)S(1)} %all-to-all-done.recv_hbm), channel_id=1, source_target_pairs={{0,1},{1,0},{2,3},{3,2},{4,5},{5,4},{6,7},{7,6},{8,9},{9,8},{10,11... | collective-permute-start | bytes 1966088 | tf_op jit(solution)/shard_map/ppermute | solution.py:313
  28.0 11.2 %shard_map.96 = (f32[8,288,256]{2,1,0:T(8,128)}, f32[288,1024]{1,0:T(8,128)S(1)}, f32[8,128]{1,0:T(8,128)S(1)}) custom-call(bf16[16,160,128]{2,1,0:T(8,128)(2,1)S(1)} %all-to-all-done.recv_hbm, bf16[16,288,128]{2,1,0:T(8,128)(2,1)} %bitcast.20, f32[16,128]{1,0:T(8,128)} %bitcast.28, bf16[16,256,128]{2,1,0:T(8,128)(2,1)} %get-tuple-element.22.lat_hbm, ...), custom_call_target="tpu_custom_call" | custom-call | flops 8589934592 | bytes 65536 | tf_op jit(solution)/shard_map/pallas_call | solution.py:383
  39.3 0.0 collective-permute-done.recv_hbm
  39.3 0.0 copy-start
  39.3 12.1 %shard_map.97 = (f32[8,288,256]{2,1,0:T(8,128)}, f32[288,1024]{1,0:T(8,128)S(1)}, f32[8,128]{1,0:T(8,128)}) custom-call(bf16[16,160,128]{2,1,0:T(8,128)(2,1)S(1)} %collective-permute-done.recv_hbm, bf16[16,288,128]{2,1,0:T(8,128)(2,1)} %bitcast.21, f32[16,128]{1,0:T(8,128)} %bitcast.29, bf16[16,256,128]{2,1,0:T(8,128)(2,1)} %get-tuple-element.22.lat_hbm, ...), custom_call_target="tpu_custom_call" | custom-call | flops 8589934592 | bytes 65536 | tf_op jit(solution)/shard_map/pallas_call | solution.py:383
  51.3 0.0 all-to-all-done.1.after.recv
  51.3 0.0 copy-done
  51.4 1.7 %shard_map.99 = bf16[16,288,128]{2,1,0:T(8,128)(2,1)} custom-call(f32[288,1024]{1,0:T(8,128)S(1)} %get-tuple-element.29.mine, f32[288,1024]{1,0:T(8,128)S(1)} %get-tuple-element.30.other, f32[288,128]{1,0:T(8,128)S(1)} %copy-done, bf16[16,4,64,128]{3,2,1,0:T(8,128)(2,1)S(1)} %all-to-all-done.1.after.recv), custom_call_target="tpu_custom_call" | custom-call | tf_op jit(solution)/shard_map/pallas_call | solution.py:425
  53.1 6.9 %all-to-all-start.2 = ((bf16[16,288,128]{2,1,0:T(8,128)(2,1)}), bf16[16,288,128]{2,1,0:T(8,128)(2,1)S(1)}, u32[]{:S(2)}, u32[]{:S(2)}) async-start(bf16[16,288,128]{2,1,0:T(8,128)(2,1)} %shard_map.99), calls=%async_computation.2 | async-start | bytes 2359296 | tf_op jit(solution)/shard_map/all_to_all | solution.py:432
  59.9 0.2 shard_map.100
  60.1 3.1 %collective-permute-start.1 = (bf16[2,64,128]{2,1,0:T(8,128)(2,1)S(1)}, bf16[2,64,128]{2,1,0:T(8,128)(2,1)S(1)}, u32[]{:S(2)}, u32[]{:S(2)}) collective-permute-start(bf16[2,64,128]{2,1,0:T(8,128)(2,1)S(1)} %get-tuple-element.34), channel_id=1, source_target_pairs={{0,64},{64,0},{128,192},{192,128},{1,65},{65,1},{129,193},{193,129... | collective-permute-start | bytes 98312 | tf_op jit(solution)/shard_map/ppermute | solution.py:434
  63.2 1.6 %collective-permute-done.1.recv = bf16[2,64,128]{2,1,0:T(8,128)(2,1)S(1)} collective-permute-done((bf16[2,64,128]{2,1,0:T(8,128)(2,1)S(1)}, bf16[2,64,128]{2,1,0:T(8,128)(2,1)S(1)}, u32[]{:S(2)}, u32[]{:S(2)}) %collective-permute-start.1) | collective-permute-done | bytes 32800 | tf_op jit(solution)/shard_map/ppermute | solution.py:434
  64.8 5.2 %collective-permute-start.2 = (bf16[64,128]{1,0:T(8,128)(2,1)S(1)}, bf16[64,128]{1,0:T(8,128)(2,1)S(1)}, u32[]{:S(2)}, u32[]{:S(2)}) collective-permute-start(bf16[64,128]{1,0:T(8,128)(2,1)S(1)} %get-tuple-element.36), channel_id=1, source_target_pairs={{0,192},{64,128},{128,64},{192,0},{1,193},{65,129},{129,65},{193,1... | collective-permute-start | bytes 49160 | tf_op jit(solution)/shard_map/ppermute | solution.py:443
  70.0 4.6 %shard_map.98 = bf16[16,288,128]{2,1,0:T(8,128)(2,1)} custom-call(f32[8,288,256]{2,1,0:T(8,128)} %get-tuple-element.21.own, f32[8,288,256]{2,1,0:T(8,128)} %get-tuple-element.26.mine, f32[8,288,256]{2,1,0:T(8,128)} %get-tuple-element.28.other), custom_call_target="tpu_custom_call" | custom-call | flops 8589934592 | bytes 12582912 | tf_op jit(solution)/shard_map/pallas_call | solution.py:444
  74.6 0.0 collective-permute-done.2.weight_recv
  74.6 3.9 %all-to-all-done.2.recv = bf16[16,288,128]{2,1,0:T(8,128)(2,1)S(1)} async-done(((bf16[16,288,128]{2,1,0:T(8,128)(2,1)}), bf16[16,288,128]{2,1,0:T(8,128)(2,1)S(1)}, u32[]{:S(2)}, u32[]{:S(2)}) %all-to-all-start.2) | async-done | bytes 1179680 | tf_op jit(solution)/shard_map/all_to_all | solution.py:432
  78.5 0.8 shard_map.102
  79.3 7.9 %all-gather = bf16[1152,128]{1,0:T(8,128)(2,1)S(1)} all-gather(bf16[288,128]{1,0:T(8,128)(2,1)S(1)} %get-tuple-element.37), channel_id=2, replica_groups=mesh['dp'=4,'ctx'=16,'head'=4] {'head'}, dimensions={0}, use_global_device_ids=true | all-gather | bytes 368640 | tf_op jit(solution)/shard_map/all_gather | solution.py:467
  87.2 0.8 shard_map.103
  (1 shorter events, 0.0 us)
Async XLA Ops:
  2.7 19.2 %all-to-all-start = ((bf16[16,160,128]{2,1,0:T(8,128)(2,1)}), bf16[16,160,128]{2,1,0:T(8,128)(2,1)S(1)}, u32[]{:S(2)}, u32[]{:S(2)}) async-start(bf16[16,160,128]{2,1,0:T(8,128)(2,1)} %shard_map.95), calls=%async_computation | async-start | bytes 1310720 | tf_op jit(solution)/shard_map/all_to_all | solution.py:330
  21.9 29.4 %all-to-all-start.1 = ((bf16[16,4,64,128]{3,2,1,0:T(8,128)(2,1)}), bf16[16,4,64,128]{3,2,1,0:T(8,128)(2,1)S(1)}, u32[]{:S(2)}, u32[]{:S(2)}) async-start(bf16[16,4,64,128]{3,2,1,0:T(8,128)(2,1)} %get-tuple-element.32), calls=%async_computation.1 | async-start | bytes 2097152 | tf_op jit(solution)/shard_map/all_to_all | solution.py:412
  26.4 12.8 %collective-permute-start = (bf16[16,160,128]{2,1,0:T(8,128)(2,1)S(1)}, bf16[16,160,128]{2,1,0:T(8,128)(2,1)S(1)}, u32[]{:S(2)}, u32[]{:S(2)}) collective-permute-start(bf16[16,160,128]{2,1,0:T(8,128)(2,1)S(1)} %all-to-all-done.recv_hbm), channel_id=1, source_target_pairs={{0,1},{1,0},{2,3},{3,2},{4,5},{5,4},{6,7},{7,6},{8,9},{9,8},{10,11... | collective-permute-start | bytes 1966088 | tf_op jit(solution)/shard_map/ppermute | solution.py:313
  39.3 12.1 %copy-start = (f32[288,128]{1,0:T(8,128)S(1)}, f32[288,128]{1,0:T(8,128)}, u32[]{:S(2)}) copy-start(f32[288,128]{1,0:T(8,128)} %get-tuple-element.31.own_ref) | copy-start | bytes 442372
  53.1 25.4 %all-to-all-start.2 = ((bf16[16,288,128]{2,1,0:T(8,128)(2,1)}), bf16[16,288,128]{2,1,0:T(8,128)(2,1)S(1)}, u32[]{:S(2)}, u32[]{:S(2)}) async-start(bf16[16,288,128]{2,1,0:T(8,128)(2,1)} %shard_map.99), calls=%async_computation.2 | async-start | bytes 2359296 | tf_op jit(solution)/shard_map/all_to_all | solution.py:432
  60.1 4.7 %collective-permute-start.1 = (bf16[2,64,128]{2,1,0:T(8,128)(2,1)S(1)}, bf16[2,64,128]{2,1,0:T(8,128)(2,1)S(1)}, u32[]{:S(2)}, u32[]{:S(2)}) collective-permute-start(bf16[2,64,128]{2,1,0:T(8,128)(2,1)S(1)} %get-tuple-element.34), channel_id=1, source_target_pairs={{0,64},{64,0},{128,192},{192,128},{1,65},{65,1},{129,193},{193,129... | collective-permute-start | bytes 98312 | tf_op jit(solution)/shard_map/ppermute | solution.py:434
  64.8 9.8 %collective-permute-start.2 = (bf16[64,128]{1,0:T(8,128)(2,1)S(1)}, bf16[64,128]{1,0:T(8,128)(2,1)S(1)}, u32[]{:S(2)}, u32[]{:S(2)}) collective-permute-start(bf16[64,128]{1,0:T(8,128)(2,1)S(1)} %get-tuple-element.36), channel_id=1, source_target_pairs={{0,192},{64,128},{128,64},{192,0},{1,193},{65,129},{129,65},{193,1... | collective-permute-start | bytes 49160 | tf_op jit(solution)/shard_map/ppermute | solution.py:443

commit v3 on v2

--- a/solution.py
+++ b/solution.py
@@ -19,9 +19,9 @@
 ROT = 2 * HALF
 RANK = ROT + HALF * ROPE // TOK
 BLOCK = RANK + 16
+SPLIT = FULL // 2
 F32 = jnp.float32
 BF16 = jnp.bfloat16
-FLOPS = (1 << 33, 1 << 33)
 NT = (((1,), (1,)), ((), ()))
 VM = pl.BlockSpec(memory_space=pltpu.VMEM)
 ANY = pl.BlockSpec(memory_space=pl.ANY)
@@ -95,10 +95,11 @@
 
 
 def prologue_kernel(out_grad_hbm, saved_hbm, up_hbm, q_hbm, lat_hbm, pos_hbm, lse_hbm, *rest):
-    start, lat_hbm_out, scaled_hbm, delta_hbm, own_hbm, query_hbm, parts_hbm = rest[:7]
-    queries, lse, lat_grad, lat_scaled, delta = rest[7:12]
-    out_grad, saved, value_up, lat_ref, pos_ref, grad_s, saved_s, part_s, parts, key_s = rest[-15:-5]
-    key_own, own_s, query_own, sem, out_sem = rest[-5:]
+    start, lat_hbm_out, scaled_hbm, delta_hbm, mine_hbm, other_hbm, query_hbm, parts_hbm = rest[:8]
+    queries, lse, lat_grad, lat_scaled, delta = rest[8:13]
+    out_grad, saved, value_up, lat_ref, pos_ref, grad_s, saved_s, part_s, parts, key_s = rest[-16:-6]
+    key_own, key_mine, key_other, query_own, sem, out_sem = rest[-6:]
+    side = lax.rem(lax.axis_index("ctx"), 2)
     core = lax.rem(lax.axis_index("head"), 2)
     moves = [
         (out_grad_hbm, out_grad),
@@ -144,7 +145,8 @@
         (lat_grad, lat_hbm_out),
         (lat_scaled, scaled_hbm),
         (delta, delta_hbm),
-        (own_s, own_hbm),
+        (key_mine, mine_hbm),
+        (key_other, other_hbm),
         (query_own, query_hbm),
     ]
     outs = [pltpu.make_async_copy(src, dst, out_sem.at[i]) for i, (src, dst) in enumerate(outs)]
@@ -167,8 +169,12 @@
         query_own[pair] = dot(lat_ref[...], dl)
         key_own[...] += dot_nt(q2, dl)
         key_own[:LATENT] += dot_nt(both(lat_grad, pair), weights.astype(BF16))
+    here = lax.broadcasted_iota(jnp.int32, (FULL, TOK), 1) // HALF == side
     own = key_own[...]
-    own_s[...] = jnp.where(core == 0, own, jnp.concatenate([own[:, HALF:], own[:, :HALF]], axis=1))
+    kept = jnp.where(here, own, 0.0)
+    moved = jnp.where(here, jnp.concatenate([own[:, HALF:], own[:, :HALF]], axis=1), 0.0)
+    key_mine[...] = jnp.where(core == side, kept, moved)
+    key_other[...] = jnp.where(core == side, moved, kept)
     for copy in outs[4:]:
         copy.start()
     for copy in outs:
@@ -176,18 +182,24 @@
 
 
 def attention_kernel(
-    recv_hbm, q_hbm, lse_hbm, lat_hbm, scaled_hbm, delta_hbm, after, query_hbm, key_acc, done,
-    recv, queries, lse, lat_grad, lat_scaled, delta, key_s, keys_t, query_s, sem, in_sem,
+    first, last, recv_hbm, pos_hbm, q_hbm, lse_hbm, lat_hbm, scaled_hbm, delta_hbm, own_hbm, so_far, after,
+    query_hbm, key_out, done,
+    recv, pos, queries, lse, lat_grad, lat_scaled, delta, key_own, key_acc, key_s, keys_t, query_s, last_s, sem, in_sem,
 ):
     heads = queries.shape[0]
     count = key_s.shape[0] // HALF
-    quarter = count // 4
-    moves = [(recv_hbm.at[i * quarter : (i + 1) * quarter], recv.at[i * quarter : (i + 1) * quarter]) for i in range(4)]
-    moves += [(lse_hbm, lse), (delta_hbm, delta)]
-    near = heads // 2
-    for lo in (0, near):
+    quarter = max(1, count // 4)
+    base = count // quarter
+    moves = []
+    for lo in range(0, count, quarter):
+        moves.append((recv_hbm.at[first + lo : first + lo + quarter], recv.at[lo : lo + quarter]))
+    moves += [(lse_hbm, lse), (delta_hbm, delta), (pos_hbm, pos)]
+    near = heads // 4
+    for lo in range(0, heads, near):
         pieces = ((q_hbm, queries), (scaled_hbm, lat_scaled), (lat_hbm, lat_grad))
         moves += [(src.at[lo : lo + near], dst.at[lo : lo + near]) for src, dst in pieces]
+        moves.append((so_far.at[lo // 2 : (lo + near) // 2], query_s.at[lo // 2 : (lo + near) // 2]))
+    moves.append((own_hbm, key_own))
     copies = [pltpu.make_async_copy(src, dst, in_sem.at[i]) for i, (src, dst) in enumerate(moves)]
     for copy in copies:
         copy.start()
@@ -202,13 +214,18 @@
         rot = recv[j, ROT:RANK].astype(F32)
         for g in range(HALF // 16):
             key_s[lo + 16 * g : lo + 16 * g + 16, LATENT:] = rot[:, ROPE * g : ROPE * g + ROPE].astype(BF16)
-        if j % 2:
-            keys_t[:, lo - HALF : lo + HALF] = key_s[lo - HALF : lo + HALF, :].T
-    rank_q = recv[own, RANK : RANK + 1, :].astype(F32)
+    copies[base + 2].wait()
+    rank_q = jnp.min(pos[...].astype(F32), axis=1, keepdims=True) * (1.0 / TOK)
     far = []
     for j in range(count):
         one_far = jnp.where(recv[j, RANK : RANK + 1, :].astype(F32) < rank_q, 0.0, FAR)
         far.append(jnp.concatenate([one_far, one_far], axis=1))
+    def copy_out(pair):
+        if last:
+            part = pl.ds(2 * pair, 2)
+            return pltpu.make_async_copy(last_s.at[part], query_hbm.at[part], sem.at[pair])
+        return pltpu.make_async_copy(query_s.at[pair], query_hbm.at[pair], sem.at[pair])
+
     def one(pair, _):
         q2 = both(queries, pair)
         logits = dot(key_s[...], q2)
@@ -223,8 +240,13 @@
             axis=0,
         )
         dl = (weights * (dot_value - delta2)).astype(BF16)
-        query_s[pair] = dot(keys_t[...], dl)
-        pltpu.make_async_copy(query_s.at[pair], query_hbm.at[pair], sem.at[pair]).start()
+        grad = query_s[pair] + dot(keys_t[...], dl)
+        if last:
+            last_s[2 * pair] = grad[:, :TOK].astype(BF16)
+            last_s[2 * pair + 1] = grad[:, TOK:].astype(BF16)
+        else:
+            query_s[pair] = grad
+        copy_out(pair).start()
         key_acc[:LATENT] += dot_nt(
             jnp.concatenate([q2[:LATENT], both(lat_grad, pair)], axis=1),
             jnp.concatenate([dl, weights.astype(BF16)], axis=1),
@@ -232,26 +254,38 @@
         key_acc[LATENT:] += dot_nt(q2[LATENT:], dl)
         return 0
 
-    for i in range(2):
-        for copy in copies[4 + 5 * i : 9 + 3 * i]:
+    for i in range(4):
+        at = base + 3 + 4 * i
+        for copy in copies[at : at + 4] if i else copies[base : base + 2] + copies[at : at + 4]:
             copy.wait()
+        if i == 0:
+            for lo in range(0, count * HALF, TOK):
+                keys_t[:, lo : lo + TOK] = key_s[lo : lo + TOK, :].T
         lax.fori_loop(near // 2 * i, near // 2 * (i + 1), one, 0, unroll=near // 2)
+    copies[-1].wait()
+    for t in range(count * HALF // TOK):
+        total = key_acc[:, TOK * t : TOK * t + TOK]
+        total = total + jnp.where(own // 2 == first // 2 + t, 1.0, 0.0) * key_own[...]
+        key_out[:, TOK * t : TOK * t + TOK] = total.astype(key_out.dtype)
     done[...] = after[: done.shape[0]]
     for pair in range(heads // 2):
-        pltpu.make_async_copy(query_s.at[pair], query_hbm.at[pair], sem.at[pair]).wait()
-
-
-def pack_kernel(mine, other, own_ref, after, out_ref):
+        copy_out(pair).wait()
+
+
+def pack_kernel(mine_1, mine_2, recv, after, out_ref):
     del after
-    own = lax.axis_index("ctx")
-    for j in range(out_ref.shape[0]):
-        lo = HALF * j
-        total = jnp.concatenate([mine[:, lo : lo + HALF], other[:, lo : lo + HALF]], axis=1)
-        total = total + jnp.where(own == j, 1.0, 0.0) * own_ref[...]
-        out_ref[j] = total.astype(BF16)
-
-
-def weight_kernel(recv, friend_ref, keep_ref):
+    t = 0
+    for ref in (mine_1, mine_2):
+        for i in range(ref.shape[1] // TOK):
+            tile = ref[:, TOK * i : TOK * i + TOK] + recv[:, TOK * t : TOK * t + TOK].astype(F32)
+            low, high = tile[:SPLIT], tile[SPLIT:]
+            out_ref[2 * t] = jnp.concatenate([low[:, :HALF], high[:, :HALF]], axis=1).astype(BF16)
+            out_ref[2 * t + 1] = jnp.concatenate([low[:, HALF:], high[:, HALF:]], axis=1).astype(BF16)
+            t += 1
+
+
+def weight_kernel(recv, after, friend_ref, keep_ref):
+    del after
     total = recv[0].astype(F32)
     for j in range(1, recv.shape[0]):
         total = total + recv[j].astype(F32)
@@ -271,18 +305,15 @@
     send_ref[...] = total[1].astype(BF16)
 
 
-def query_kernel(own, mine, other, out_ref):
-    for i in range(own.shape[0]):
-        grad = own[i] + mine[i] + other[i]
-        out_ref[2 * i] = grad[:, :TOK].astype(BF16)
-        out_ref[2 * i + 1] = grad[:, TOK:].astype(BF16)
-
-
-def sum_kernel(recv, stay, weight_recv, key_ref, weight_ref, part_s):
+def sum_kernel(recv, key_ref):
     total = recv[0].astype(F32)
     for j in range(1, recv.shape[0]):
         total = total + recv[j].astype(F32)
     key_ref[...] = total.astype(BF16)
+
+
+def share_kernel(stay, weight_recv, after, weight_ref, part_s):
+    del after
     part_s[...] = stay[...] + weight_recv[...].astype(F32)
     width, heads = weight_ref.shape[0], weight_ref.shape[1]
     for i in range(width):
@@ -296,7 +327,8 @@
         for other in range(core + 2, parts.shape[0], 2):
             total = total + parts[other].astype(F32)
         sides.append(total)
-    out_ref[...] = sides[0] + jnp.concatenate([sides[1][:, HALF:], sides[1][:, :HALF]], axis=1)
+    out_ref[:SPLIT] = jnp.concatenate([sides[0][:, :HALF], sides[1][:, :HALF]], axis=1)
+    out_ref[SPLIT:] = jnp.concatenate([sides[0][:, HALF:], sides[1][:, HALF:]], axis=1)
 
 
 def body(queries, latents, positions, lse, saved_out, out_grad, value_up):
@@ -330,7 +362,7 @@
     recv_mine = lax.all_to_all(payload, "ctx", 0, 0)
 
     part_rows = heads * width
-    start, lat_grad, lat_scaled, delta, key_own, query_own, parts = pl.pallas_call(
+    start, lat_grad, lat_scaled, delta, key_mine, key_other, query_own, parts = pl.pallas_call(
         prologue_kernel,
         out_shape=[
             near_shape((8, TOK), F32),
@@ -338,11 +370,12 @@
             far_shape((heads, LATENT, TOK), BF16),
             far_shape((heads, TOK), F32),
             far_shape((FULL, TOK), F32),
+            far_shape((FULL, TOK), F32),
             far_shape((pairs, FULL, 2 * TOK), F32),
             far_shape((n_ctx, n_dp, part_rows, VHEAD), BF16),
         ],
         in_specs=[ANY] * 7,
-        out_specs=[VM] + [ANY] * 6,
+        out_specs=[VM] + [ANY] * 7,
         scratch_shapes=[
             pltpu.VMEM((heads, FULL, TOK), BF16),
             pltpu.VMEM((heads, TOK), F32),
@@ -361,9 +394,10 @@
             pltpu.VMEM((TOK, FULL), BF16),
             pltpu.VMEM((FULL, TOK), F32),
             pltpu.VMEM((FULL, TOK), F32),
+            pltpu.VMEM((FULL, TOK), F32),
             pltpu.VMEM((pairs, FULL, 2 * TOK), F32),
             pltpu.SemaphoreType.DMA((7,)),
-            pltpu.SemaphoreType.DMA((6,)),
+            pltpu.SemaphoreType.DMA((7,)),
         ],
         compiler_params=vmem(28),
         cost_estimate=cost(2 * heads * TOK * TOK * 1900, 8 << 20, heads * TOK * TOK),
@@ -378,58 +412,68 @@
     )
     recv_other = core_swap(recv_mine)
 
-    def attend(recv, after, flops):
-        rows = n_ctx * HALF
+    def attend(recv, first, count, other, last, so_far, after):
+        rows = count * HALF
         return pl.pallas_call(
-            attention_kernel,
+            functools.partial(attention_kernel, first, last),
             out_shape=[
-                far_shape((pairs, FULL, 2 * TOK), F32),
-                near_shape((FULL, rows), F32),
+                shape((heads, FULL, TOK), BF16) if last else far_shape((pairs, FULL, 2 * TOK), F32),
+                shape((FULL, rows), BF16) if other else near_shape((FULL, rows), F32),
                 near_shape((8, TOK), F32),
             ],
-            in_specs=[ANY] * 6 + [VM],
+            in_specs=[ANY] * 9 + [VM],
             out_specs=[ANY, VM, VM],
             scratch_shapes=[
-                pltpu.VMEM((n_ctx, BLOCK, TOK), BF16),
+                pltpu.VMEM((count, BLOCK, TOK), BF16),
+                pltpu.VMEM((1, TOK), jnp.int32),
                 pltpu.VMEM((heads, FULL, TOK), BF16),
                 pltpu.VMEM((heads, TOK), F32),
                 pltpu.VMEM((heads, LATENT, TOK), BF16),
                 pltpu.VMEM((heads, LATENT, TOK), BF16),
                 pltpu.VMEM((heads, TOK), F32),
+                pltpu.VMEM((FULL, TOK), F32),
+                pltpu.VMEM((FULL, rows), F32),
                 pltpu.VMEM((rows, FULL), BF16),
                 pltpu.VMEM((FULL, rows), BF16),
                 pltpu.VMEM((pairs, FULL, 2 * TOK), F32),
+                pltpu.VMEM((heads, FULL, TOK), BF16),
                 pltpu.SemaphoreType.DMA((pairs,)),
-                pltpu.SemaphoreType.DMA((12,)),
+                pltpu.SemaphoreType.DMA((24,)),
             ],
             compiler_params=vmem(24),
-            cost_estimate=cost(flops, 1 << 16),
-        )(recv, q_t, lse_t, far_away(lat_grad), far_away(lat_scaled), far_away(delta), held(after))
-
-    query_1, sum_1, step = attend(recv_mine, start, FLOPS[0])
-    query_2, sum_2, step = attend(recv_other, step, FLOPS[1])
+            cost_estimate=cost(1 << 33, 1 << 16),
+        )(
+            recv, positions, q_t, lse_t, far_away(lat_grad), far_away(lat_scaled), far_away(delta),
+            far_away(key_other if other else key_mine), far_away(so_far), held(after),
+        )
+
+    near = n_ctx // 2
+    query, sum_1, step = attend(recv_mine, 0, near, False, False, query_own, start)
+    query, sum_2, step = attend(recv_other, 0, n_ctx, True, False, query, step)
+    sum_recv = core_swap(sum_2)
+    query_grad, sum_3, step = attend(recv_mine, near, n_ctx - near, False, True, query, step)
 
     weight_ctx = lax.all_to_all(parts, "ctx", 0, 0)
+    packed = pl.pallas_call(
+        pack_kernel,
+        out_shape=shape((n_ctx, SPLIT, TOK), BF16),
+        in_specs=[VM] * 3 + [ANY],
+        out_specs=VM,
+        compiler_params=vmem(6),
+    )(held(sum_1), held(sum_3), sum_recv, weight_ctx)
+    summed = lax.all_to_all(packed, "ctx", 0, 0)
+
     send_1, keep_1 = pl.pallas_call(
         weight_kernel,
         out_shape=[
             shape((2, part_rows, VHEAD), BF16),
             shape((2, part_rows, VHEAD), BF16),
         ],
-        in_specs=[VM],
+        in_specs=[VM, ANY],
         out_specs=[VM] * 2,
         compiler_params=vmem(4),
         cost_estimate=cost(1 << 16, 1 << 16),
-    )(weight_ctx)
-
-    packed = pl.pallas_call(
-        pack_kernel,
-        out_shape=shape((n_ctx, FULL, TOK), BF16),
-        in_specs=[VM] * 3 + [ANY],
-        out_specs=VM,
-        compiler_params=vmem(6),
-    )(held(sum_1), held(sum_2), key_own, weight_ctx)
-    summed = lax.all_to_all(packed, "ctx", 0, 0)
+    )(weight_ctx, packed)
 
     recv_1 = lax.ppermute(send_1, "dp", [(i, i ^ 1) for i in range(n_dp)])
     stay, send_2 = pl.pallas_call(
@@ -441,23 +485,22 @@
         cost_estimate=cost(1 << 16, 1 << 16),
     )(keep_1, recv_1)
     recv_2 = lax.ppermute(send_2, "dp", [(i, n_dp - 1 - i) for i in range(n_dp)])
-    query_grad = pl.pallas_call(
-        query_kernel,
-        out_shape=shape((heads, FULL, TOK), BF16),
-        grid=(4,),
-        in_specs=[pl.BlockSpec((pairs // 4, FULL, 2 * TOK), lambda p: (p, 0, 0))] * 3,
-        out_specs=pl.BlockSpec((heads // 4, FULL, TOK), lambda p: (p, 0, 0)),
-        compiler_params=vmem(12),
-        cost_estimate=cost(1 << 33, 12 << 20),
-    )(*[far_away(x) for x in (query_own, query_1, query_2)])
-    key_part, weight_share = pl.pallas_call(
+    key_part = pl.pallas_call(
         sum_kernel,
-        out_shape=[shape((FULL, TOK), BF16), shape((width, heads, VHEAD), F32)],
-        in_specs=[VM] * 3,
-        out_specs=[VM] * 2,
+        out_shape=shape((SPLIT, TOK), BF16),
+        in_specs=[VM],
+        out_specs=VM,
+        compiler_params=vmem(4),
+    )(summed)
+    weight_share = pl.pallas_call(
+        share_kernel,
+        out_shape=shape((width, heads, VHEAD), F32),
+        in_specs=[VM] * 2 + [ANY],
+        out_specs=VM,
         scratch_shapes=[pltpu.VMEM((heads * width, VHEAD), F32)],
-        compiler_params=vmem(4),
-    )(summed, stay, recv_2)
+        compiler_params=vmem(2),
+        cost_estimate=cost(1 << 16, 1 << 16),
+    )(stay, recv_2, key_part)
     key_grad = pl.pallas_call(
         last_kernel,
         out_shape=shape((FULL, TOK), F32),

time: 88.5 us -> 85.6 us (0.967)
  waiting for transfers between devices: 7.68 us -> 4.31 us
    all_to_all x1, waiting for transfers between devices: 3.9 us -> 0.88 us  [body(): summed = lax.all_to_all(packed, 'ctx', 0, 0)]
    ppermute x1 -> x2, starting transfers between devices: 1.59 us -> 2.13 us  [core_swap(): return lax.ppermute(x, 'head', [(i, i ^ 1) for i in range(n_head)])]
    pallas_call x5 -> x6, Pallas kernels: 30.4 us -> 30.5 us  [the longest x3 28.7 us: attend(): pl.pallas_call(functools.partial(attention_kernel, first, last), out_shap...]
  transfers between devices with their start and end apart: 6 -> 7, of which waited for: 3 -> 3; matrix products, arithmetic and copies ran while one was open for 0% -> 0% of each run, Pallas kernels for 43% -> 46%
where the time goes in v3:
time: 85.6 us; the launch traced here: 85.2 us
  Pallas kernels  43 us (50%)
  starting transfers between devices  29.5 us (34%)
  blocking collectives  7.62 us (9%)
  waiting for transfers between devices  4.31 us (5%)
    pallas_call x3, Pallas kernels, attend(): pl.pallas_call(functools.partial(attention_kernel, first, last), out_shap...  28.7 us
    pallas_call x1, Pallas kernels, body(): pl.pallas_call(prologue_kernel, out_shape=[near_shape((8, TOK), F32), far...  9.48 us
    all_gather x1, blocking collectives, body(): lax.all_gather(key_part, 'head')  7.62 us
    all_to_all x1, starting transfers between devices, body(): recv_mine = lax.all_to_all(payload, 'ctx', 0, 0)  7.6 us
    all_to_all x1, starting transfers between devices, body(): summed = lax.all_to_all(packed, 'ctx', 0, 0)  6.68 us
    ppermute x1, starting transfers between devices, body(): lax.ppermute(send_2, 'dp', [(i, n_dp - 1 - i) for i in range(n_dp)])  5.48 us
    all_to_all x1, starting transfers between devices, body(): weight_ctx = lax.all_to_all(parts, 'ctx', 0, 0)  4.56 us
    ppermute x1, starting transfers between devices, body(): recv_1 = lax.ppermute(send_1, 'dp', [(i, i ^ 1) for i in range(n_dp)])  3.07 us
  transfers between devices with their start and end apart: 7, of which 3 were waited for; matrix products, arithmetic and copies ran while one was open for 0% of the time, Pallas kernels for 46%

profile of v3, /device:TPU:1, one launch (start us, length us, event | category | flops | bytes accessed | tf_op | source)
XLA Modules:
  0.0 85.2 jit_solution(5400587604105097297)
XLA Ops:
  0.6 2.0 %shard_map.94 = bf16[16,160,128]{2,1,0:T(8,128)(2,1)} custom-call(bf16[288,128]{1,0:T(8,128)(2,1)} %bitcast.25, s32[1,128]{1,0:T(1,128)} %pos_hbm.9), custom_call_target="tpu_custom_call" | custom-call | tf_op jit(solution)/shard_map/pallas_call | solution.py:347
  2.7 7.6 %all-to-all-start = ((bf16[16,160,128]{2,1,0:T(8,128)(2,1)}), bf16[16,160,128]{2,1,0:T(8,128)(2,1)S(1)}, u32[]{:S(2)}, u32[]{:S(2)}) async-start(bf16[16,160,128]{2,1,0:T(8,128)(2,1)} %shard_map.94), calls=%async_computation | async-start | bytes 1310720 | tf_op jit(solution)/shard_map/all_to_all | solution.py:362
  10.3 9.5 %shard_map.95 = (f32[8,128]{1,0:T(8,128)S(1)}, bf16[16,256,128]{2,1,0:T(8,128)(2,1)}, bf16[16,256,128]{2,1,0:T(8,128)(2,1)}, f32[16,128]{1,0:T(8,128)}, f32[288,...) custom-call(bf16[2048,128]{1,0:T(8,128)(2,1)} %bitcast.24, ...), custom_call_target="tpu_custom_call" | custom-call | flops 996147200 | bytes 8388608 | tf_op jit(solution)/shard_map/pallas_call | solution.py:365
  19.8 2.1 %all-to-all-done.recv_hbm = bf16[16,160,128]{2,1,0:T(8,128)(2,1)S(1)} async-done(((bf16[16,160,128]{2,1,0:T(8,128)(2,1)}), bf16[16,160,128]{2,1,0:T(8,128)(2,1)S(1)}, u32[]{:S(2)}, u32[]{:S(2)}) %all-to-all-start) | async-done | bytes 655392 | tf_op jit(solution)/shard_map/all_to_all | solution.py:362
  21.9 4.6 %all-to-all-start.1 = ((bf16[16,4,64,128]{3,2,1,0:T(8,128)(2,1)}), bf16[16,4,64,128]{3,2,1,0:T(8,128)(2,1)S(1)}, u32[]{:S(2)}, u32[]{:S(2)}) async-start(bf16[16,4,64,128]{3,2,1,0:T(8,128)(2,1)} %get-tuple-element.38), calls=%async_computation.1 | async-start | bytes 2097152 | tf_op jit(solution)/shard_map/all_to_all | solution.py:456
  26.4 1.8 %collective-permute-start = (bf16[16,160,128]{2,1,0:T(8,128)(2,1)S(1)}, bf16[16,160,128]{2,1,0:T(8,128)(2,1)S(1)}, u32[]{:S(2)}, u32[]{:S(2)}) collective-permute-start(bf16[16,160,128]{2,1,0:T(8,128)(2,1)S(1)} %all-to-all-done.recv_hbm), channel_id=1, source_target_pairs={{0,1},{1,0},{2,3},{3,2},{4,5},{5,4},{6,7},{7,6},{8,9},{9,8},{10,11... | collective-permute-start | bytes 1966088 | tf_op jit(solution)/shard_map/ppermute | solution.py:345
  28.2 7.8 %shard_map.96 = (f32[8,288,256]{2,1,0:T(8,128)}, f32[288,512]{1,0:T(8,128)S(1)}, f32[8,128]{1,0:T(8,128)S(1)}) custom-call(bf16[16,160,128]{2,1,0:T(8,128)(2,1)S(1)} %all-to-all-done.recv_hbm, s32[1,128]{1,0:T(1,128)} %pos_hbm.9, bf16[16,288,128]{2,1,0:T(8,128)(2,1)} %bitcast.20, f32[16,128]{1,0:T(8,128)} %bitcast.29, ...), custom_call_target="tpu_custom_call" | custom-call | flops 8589934592 | bytes 65536 | tf_op jit(solution)/shard_map/pallas_call | solution.py:417
  36.0 0.0 collective-permute-done.recv_hbm
  36.0 12.7 %shard_map.97 = (f32[8,288,256]{2,1,0:T(8,128)}, bf16[288,1024]{1,0:T(8,128)(2,1)}, f32[8,128]{1,0:T(8,128)S(1)}) custom-call(bf16[16,160,128]{2,1,0:T(8,128)(2,1)S(1)} %collective-permute-done.recv_hbm, s32[1,128]{1,0:T(1,128)} %pos_hbm.9, bf16[16,288,128]{2,1,0:T(8,128)(2,1)} %bitcast.21, f32[16,128]{1,0:T(8,128)} %bitcast.30, ...), custom_call_target="tpu_custom_call" | custom-call | flops 8589934592 | bytes 65536 | tf_op jit(solution)/shard_map/pallas_call | solution.py:417
  48.7 0.4 collective-permute-start.1
  49.0 8.3 %shard_map.98 = (bf16[16,288,128]{2,1,0:T(8,128)(2,1)}, f32[288,512]{1,0:T(8,128)S(1)}, f32[8,128]{1,0:T(8,128)}) custom-call(bf16[16,160,128]{2,1,0:T(8,128)(2,1)S(1)} %all-to-all-done.recv_hbm, s32[1,128]{1,0:T(1,128)} %pos_hbm.9, bf16[16,288,128]{2,1,0:T(8,128)(2,1)} %bitcast.22, f32[16,128]{1,0:T(8,128)} %bitcast.31, ...), custom_call_target="tpu_custom_call" | custom-call | flops 8589934592 | bytes 65536 | tf_op jit(solution)/shard_map/pallas_call | solution.py:417
  57.4 0.0 all-to-all-done.1.after.recv
  57.4 0.0 collective-permute-done.1.recv
  57.4 1.1 %shard_map.99.after = bf16[16,144,128]{2,1,0:T(8,128)(2,1)} custom-call(f32[288,512]{1,0:T(8,128)S(1)} %get-tuple-element.35.mine_1, f32[288,512]{1,0:T(8,128)S(1)} %get-tuple-element.36.mine_2, bf16[288,1024]{1,0:T(8,128)(2,1)S(1)} %collective-permute-done.1.recv, bf16[16,4,64,128]{3,2,1,0:T(8,128)(2,1)S(1)} %all-to-all-done.1.after.recv), custom_call_target="tpu_custom_call" | custom-call | tf_op jit(solution)/shard_map/pallas_call | solution.py:457
  58.5 6.7 %all-to-all-start.2 = ((bf16[16,144,128]{2,1,0:T(8,128)(2,1)}), bf16[16,144,128]{2,1,0:T(8,128)(2,1)S(1)}, u32[]{:S(2)}, u32[]{:S(2)}) async-start(bf16[16,144,128]{2,1,0:T(8,128)(2,1)} %shard_map.99.after), calls=%async_computation.2 | async-start | bytes 1179648 | tf_op jit(solution)/shard_map/all_to_all | solution.py:464
  65.2 0.2 shard_map.102
  65.3 3.1 %collective-permute-start.2 = (bf16[2,64,128]{2,1,0:T(8,128)(2,1)S(1)}, bf16[2,64,128]{2,1,0:T(8,128)(2,1)S(1)}, u32[]{:S(2)}, u32[]{:S(2)}) collective-permute-start(bf16[2,64,128]{2,1,0:T(8,128)(2,1)S(1)} %get-tuple-element.40), channel_id=1, source_target_pairs={{0,64},{64,0},{128,192},{192,128},{1,65},{65,1},{129,193},{193,129... | collective-permute-start | bytes 98312 | tf_op jit(solution)/shard_map/ppermute | solution.py:478
  68.4 1.3 %collective-permute-done.2.recv = bf16[2,64,128]{2,1,0:T(8,128)(2,1)S(1)} collective-permute-done((bf16[2,64,128]{2,1,0:T(8,128)(2,1)S(1)}, bf16[2,64,128]{2,1,0:T(8,128)(2,1)S(1)}, u32[]{:S(2)}, u32[]{:S(2)}) %collective-permute-start.2) | collective-permute-done | bytes 32800 | tf_op jit(solution)/shard_map/ppermute | solution.py:478
  69.7 5.5 %collective-permute-start.3 = (bf16[64,128]{1,0:T(8,128)(2,1)S(1)}, bf16[64,128]{1,0:T(8,128)(2,1)S(1)}, u32[]{:S(2)}, u32[]{:S(2)}) collective-permute-start(bf16[64,128]{1,0:T(8,128)(2,1)S(1)} %get-tuple-element.42), channel_id=1, source_target_pairs={{0,192},{64,128},{128,64},{192,0},{1,193},{65,129},{129,65},{193,1... | collective-permute-start | bytes 49160 | tf_op jit(solution)/shard_map/ppermute | solution.py:487
  75.2 0.9 %all-to-all-done.2.recv = bf16[16,144,128]{2,1,0:T(8,128)(2,1)S(1)} async-done(((bf16[16,144,128]{2,1,0:T(8,128)(2,1)}), bf16[16,144,128]{2,1,0:T(8,128)(2,1)S(1)}, u32[]{:S(2)}, u32[]{:S(2)}) %all-to-all-start.2) | async-done | bytes 589856 | tf_op jit(solution)/shard_map/all_to_all | solution.py:464
  76.1 0.1 shard_map.100.after
  76.2 7.6 %all-gather = bf16[576,128]{1,0:T(8,128)(2,1)S(1)} all-gather(bf16[144,128]{1,0:T(8,128)(2,1)S(1)} %shard_map.100.after), channel_id=2, replica_groups=mesh['dp'=4,'ctx'=16,'head'=4] {'head'}, dimensions={0}, use_global_device_ids=true | all-gather | bytes 184320 | tf_op jit(solution)/shard_map/all_gather | solution.py:510
  83.8 0.8 shard_map.101
  84.5 0.0 collective-permute-done.3.weight_recv
  84.5 0.6 shard_map.104
  (1 shorter events, 0.0 us)
Async XLA Ops:
  2.7 19.2 %all-to-all-start = ((bf16[16,160,128]{2,1,0:T(8,128)(2,1)}), bf16[16,160,128]{2,1,0:T(8,128)(2,1)S(1)}, u32[]{:S(2)}, u32[]{:S(2)}) async-start(bf16[16,160,128]{2,1,0:T(8,128)(2,1)} %shard_map.94), calls=%async_computation | async-start | bytes 1310720 | tf_op jit(solution)/shard_map/all_to_all | solution.py:362
  21.9 35.5 %all-to-all-start.1 = ((bf16[16,4,64,128]{3,2,1,0:T(8,128)(2,1)}), bf16[16,4,64,128]{3,2,1,0:T(8,128)(2,1)S(1)}, u32[]{:S(2)}, u32[]{:S(2)}) async-start(bf16[16,4,64,128]{3,2,1,0:T(8,128)(2,1)} %get-tuple-element.38), calls=%async_computation.1 | async-start | bytes 2097152 | tf_op jit(solution)/shard_map/all_to_all | solution.py:456
  26.4 9.6 %collective-permute-start = (bf16[16,160,128]{2,1,0:T(8,128)(2,1)S(1)}, bf16[16,160,128]{2,1,0:T(8,128)(2,1)S(1)}, u32[]{:S(2)}, u32[]{:S(2)}) collective-permute-start(bf16[16,160,128]{2,1,0:T(8,128)(2,1)S(1)} %all-to-all-done.recv_hbm), channel_id=1, source_target_pairs={{0,1},{1,0},{2,3},{3,2},{4,5},{5,4},{6,7},{7,6},{8,9},{9,8},{10,11... | collective-permute-start | bytes 1966088 | tf_op jit(solution)/shard_map/ppermute | solution.py:345
  48.7 8.7 %collective-permute-start.1 = (bf16[288,1024]{1,0:T(8,128)(2,1)}, bf16[288,1024]{1,0:T(8,128)(2,1)S(1)}, u32[]{:S(2)}, u32[]{:S(2)}) collective-permute-start(bf16[288,1024]{1,0:T(8,128)(2,1)} %get-tuple-element.37), channel_id=1, source_target_pairs={{0,1},{1,0},{2,3},{3,2},{4,5},{5,4},{6,7},{7,6},{8,9},{9,8},{10,11... | collective-permute-start | bytes 1769480 | tf_op jit(solution)/shard_map/ppermute | solution.py:345
  58.5 17.6 %all-to-all-start.2 = ((bf16[16,144,128]{2,1,0:T(8,128)(2,1)}), bf16[16,144,128]{2,1,0:T(8,128)(2,1)S(1)}, u32[]{:S(2)}, u32[]{:S(2)}) async-start(bf16[16,144,128]{2,1,0:T(8,128)(2,1)} %shard_map.99.after), calls=%async_computation.2 | async-start | bytes 1179648 | tf_op jit(solution)/shard_map/all_to_all | solution.py:464
  65.3 4.4 %collective-permute-start.2 = (bf16[2,64,128]{2,1,0:T(8,128)(2,1)S(1)}, bf16[2,64,128]{2,1,0:T(8,128)(2,1)S(1)}, u32[]{:S(2)}, u32[]{:S(2)}) collective-permute-start(bf16[2,64,128]{2,1,0:T(8,128)(2,1)S(1)} %get-tuple-element.40), channel_id=1, source_target_pairs={{0,64},{64,0},{128,192},{192,128},{1,65},{65,1},{129,193},{193,129... | collective-permute-start | bytes 98312 | tf_op jit(solution)/shard_map/ppermute | solution.py:478
  69.7 14.8 %collective-permute-start.3 = (bf16[64,128]{1,0:T(8,128)(2,1)S(1)}, bf16[64,128]{1,0:T(8,128)(2,1)S(1)}, u32[]{:S(2)}, u32[]{:S(2)}) collective-permute-start(bf16[64,128]{1,0:T(8,128)(2,1)S(1)} %get-tuple-element.42), channel_id=1, source_target_pairs={{0,192},{64,128},{128,64},{192,0},{1,193},{65,129},{129,65},{193,1... | collective-permute-start | bytes 49160 | tf_op jit(solution)/shard_map/ppermute | solution.py:487

commit v4 on v3

--- a/solution.py
+++ b/solution.py
@@ -181,50 +181,58 @@
         copy.wait()
 
 
-def attention_kernel(
-    first, last, recv_hbm, pos_hbm, q_hbm, lse_hbm, lat_hbm, scaled_hbm, delta_hbm, own_hbm, so_far, after,
-    query_hbm, key_out, done,
-    recv, pos, queries, lse, lat_grad, lat_scaled, delta, key_own, key_acc, key_s, keys_t, query_s, last_s, sem, in_sem,
-):
+def attention_kernel(first, last, stage, *rest):
+    recv_hbm, pos_hbm, *operands, own_hbm, so_far, after = rest[:10]
+    query_out, key_out, done = rest[10:13]
+    recv, pos, key_own, key_acc, key_s, keys_t, last_s, sem, in_sem = rest[-9:]
+    queries, lse, lat_grad, lat_scaled, delta = rest[13:18] if stage else operands
     heads = queries.shape[0]
     count = key_s.shape[0] // HALF
     quarter = max(1, count // 4)
-    base = count // quarter
-    moves = []
-    for lo in range(0, count, quarter):
-        moves.append((recv_hbm.at[first + lo : first + lo + quarter], recv.at[lo : lo + quarter]))
-    moves += [(lse_hbm, lse), (delta_hbm, delta), (pos_hbm, pos)]
+    copies = []
+
+    def fetch(src, dst):
+        copies.append(pltpu.make_async_copy(src, dst, in_sem.at[len(copies)]))
+        copies[-1].start()
+        return copies[-1]
+
+    key_copies = [
+        fetch(recv_hbm.at[first + lo : first + lo + quarter], recv.at[lo : lo + quarter])
+        for lo in range(0, count, quarter)
+    ]
+    pos_copy = fetch(pos_hbm, pos)
     near = heads // 4
-    for lo in range(0, heads, near):
-        pieces = ((q_hbm, queries), (scaled_hbm, lat_scaled), (lat_hbm, lat_grad))
-        moves += [(src.at[lo : lo + near], dst.at[lo : lo + near]) for src, dst in pieces]
-        moves.append((so_far.at[lo // 2 : (lo + near) // 2], query_s.at[lo // 2 : (lo + near) // 2]))
-    moves.append((own_hbm, key_own))
-    copies = [pltpu.make_async_copy(src, dst, in_sem.at[i]) for i, (src, dst) in enumerate(moves)]
-    for copy in copies:
-        copy.start()
+    groups = [[fetch(operands[1], lse), fetch(operands[4], delta)] if stage else []] + [[], [], []]
+    for i in range(4):
+        part = slice(near * i, near * i + near)
+        if stage:
+            groups[i] += [
+                fetch(src.at[part], dst.at[part])
+                for src, dst in ((operands[0], queries), (operands[3], lat_scaled), (operands[2], lat_grad))
+            ]
+            half = slice(near // 2 * i, near // 2 * (i + 1))
+            groups[i].append(fetch(so_far.at[half], query_out.at[half]))
+    own_copy = fetch(own_hbm, key_own)
     own = lax.axis_index("ctx")
     key_acc[...] = jnp.zeros_like(key_acc)
     for j in range(count):
         if j % quarter == 0:
-            copies[j // quarter].wait()
+            key_copies[j // quarter].wait()
         lo = HALF * j
         key_s[lo : lo + HALF, :TOK] = recv[j, :HALF]
         key_s[lo : lo + HALF, TOK:LATENT] = recv[j, HALF:ROT]
         rot = recv[j, ROT:RANK].astype(F32)
         for g in range(HALF // 16):
             key_s[lo + 16 * g : lo + 16 * g + 16, LATENT:] = rot[:, ROPE * g : ROPE * g + ROPE].astype(BF16)
-    copies[base + 2].wait()
+    pos_copy.wait()
     rank_q = jnp.min(pos[...].astype(F32), axis=1, keepdims=True) * (1.0 / TOK)
     far = []
     for j in range(count):
         one_far = jnp.where(recv[j, RANK : RANK + 1, :].astype(F32) < rank_q, 0.0, FAR)
         far.append(jnp.concatenate([one_far, one_far], axis=1))
     def copy_out(pair):
-        if last:
-            part = pl.ds(2 * pair, 2)
-            return pltpu.make_async_copy(last_s.at[part], query_hbm.at[part], sem.at[pair])
-        return pltpu.make_async_copy(query_s.at[pair], query_hbm.at[pair], sem.at[pair])
+        part = pl.ds(2 * pair, 2)
+        return pltpu.make_async_copy(last_s.at[part], query_out.at[part], sem.at[pair])
 
     def one(pair, _):
         q2 = both(queries, pair)
@@ -240,13 +248,13 @@
             axis=0,
         )
         dl = (weights * (dot_value - delta2)).astype(BF16)
-        grad = query_s[pair] + dot(keys_t[...], dl)
+        grad = (query_out if stage else so_far)[pair] + dot(keys_t[...], dl)
         if last:
             last_s[2 * pair] = grad[:, :TOK].astype(BF16)
             last_s[2 * pair + 1] = grad[:, TOK:].astype(BF16)
+            copy_out(pair).start()
         else:
-            query_s[pair] = grad
-        copy_out(pair).start()
+            query_out[pair] = grad
         key_acc[:LATENT] += dot_nt(
             jnp.concatenate([q2[:LATENT], both(lat_grad, pair)], axis=1),
             jnp.concatenate([dl, weights.astype(BF16)], axis=1),
@@ -254,22 +262,23 @@
         key_acc[LATENT:] += dot_nt(q2[LATENT:], dl)
         return 0
 
-    for i in range(4):
-        at = base + 3 + 4 * i
-        for copy in copies[at : at + 4] if i else copies[base : base + 2] + copies[at : at + 4]:
+    for lo in range(0, count * HALF, TOK):
+        keys_t[:, lo : lo + TOK] = key_s[lo : lo + TOK, :].T
+    steps = 4 if stage else 1
+    for i in range(steps):
+        for copy in groups[i]:
             copy.wait()
-        if i == 0:
-            for lo in range(0, count * HALF, TOK):
-                keys_t[:, lo : lo + TOK] = key_s[lo : lo + TOK, :].T
-        lax.fori_loop(near // 2 * i, near // 2 * (i + 1), one, 0, unroll=near // 2)
-    copies[-1].wait()
+        each = heads // 2 // steps
+        lax.fori_loop(each * i, each * i + each, one, 0, unroll=each)
+    own_copy.wait()
     for t in range(count * HALF // TOK):
         total = key_acc[:, TOK * t : TOK * t + TOK]
         total = total + jnp.where(own // 2 == first // 2 + t, 1.0, 0.0) * key_own[...]
         key_out[:, TOK * t : TOK * t + TOK] = total.astype(key_out.dtype)
     done[...] = after[: done.shape[0]]
-    for pair in range(heads // 2):
-        copy_out(pair).wait()
+    if last:
+        for pair in range(heads // 2):
+            copy_out(pair).wait()
 
 
 def pack_kernel(mine_1, mine_2, recv, after, out_ref):
@@ -412,46 +421,52 @@
     )
     recv_other = core_swap(recv_mine)
 
-    def attend(recv, first, count, other, last, so_far, after):
+    held_shapes = [
+        ((heads, FULL, TOK), BF16),
+        ((heads, TOK), F32),
+        ((heads, LATENT, TOK), BF16),
+        ((heads, LATENT, TOK), BF16),
+        ((heads, TOK), F32),
+    ]
+
+    def attend(recv, first, count, other, stage, last, operands, so_far, after):
         rows = count * HALF
         return pl.pallas_call(
-            functools.partial(attention_kernel, first, last),
+            functools.partial(attention_kernel, first, last, stage),
             out_shape=[
-                shape((heads, FULL, TOK), BF16) if last else far_shape((pairs, FULL, 2 * TOK), F32),
+                shape((heads, FULL, TOK), BF16) if last else near_shape((pairs, FULL, 2 * TOK), F32),
                 shape((FULL, rows), BF16) if other else near_shape((FULL, rows), F32),
                 near_shape((8, TOK), F32),
-            ],
-            in_specs=[ANY] * 9 + [VM],
-            out_specs=[ANY, VM, VM],
+            ]
+            + [near_shape(*h) for h in held_shapes if stage],
+            in_specs=[ANY] * 2 + [ANY if stage else VM] * 5 + [ANY, ANY if stage else VM, VM],
+            out_specs=[ANY if last else VM, VM, VM] + [VM] * (5 if stage else 0),
             scratch_shapes=[
                 pltpu.VMEM((count, BLOCK, TOK), BF16),
                 pltpu.VMEM((1, TOK), jnp.int32),
-                pltpu.VMEM((heads, FULL, TOK), BF16),
-                pltpu.VMEM((heads, TOK), F32),
-                pltpu.VMEM((heads, LATENT, TOK), BF16),
-                pltpu.VMEM((heads, LATENT, TOK), BF16),
-                pltpu.VMEM((heads, TOK), F32),
                 pltpu.VMEM((FULL, TOK), F32),
                 pltpu.VMEM((FULL, rows), F32),
                 pltpu.VMEM((rows, FULL), BF16),
                 pltpu.VMEM((FULL, rows), BF16),
-                pltpu.VMEM((pairs, FULL, 2 * TOK), F32),
                 pltpu.VMEM((heads, FULL, TOK), BF16),
                 pltpu.SemaphoreType.DMA((pairs,)),
                 pltpu.SemaphoreType.DMA((24,)),
             ],
-            compiler_params=vmem(24),
+            input_output_aliases={} if stage or last else {8: 0},
+            compiler_params=vmem(20),
             cost_estimate=cost(1 << 33, 1 << 16),
         )(
-            recv, positions, q_t, lse_t, far_away(lat_grad), far_away(lat_scaled), far_away(delta),
-            far_away(key_other if other else key_mine), far_away(so_far), held(after),
+            recv, positions, *[far_away(x) if stage else held(x) for x in operands],
+            far_away(key_other if other else key_mine), far_away(so_far) if stage else held(so_far), held(after),
         )
 
     near = n_ctx // 2
-    query, sum_1, step = attend(recv_mine, 0, near, False, False, query_own, start)
-    query, sum_2, step = attend(recv_other, 0, n_ctx, True, False, query, step)
+    query, sum_1, step, *staged = attend(
+        recv_mine, 0, near, False, True, False, (q_t, lse_t, lat_grad, lat_scaled, delta), query_own, start
+    )
+    query, sum_2, step = attend(recv_other, 0, n_ctx, True, False, False, staged, query, step)
     sum_recv = core_swap(sum_2)
-    query_grad, sum_3, step = attend(recv_mine, near, n_ctx - near, False, True, query, step)
+    query_grad, sum_3, step = attend(recv_mine, near, n_ctx - near, False, False, True, staged, query, step)
 
     weight_ctx = lax.all_to_all(parts, "ctx", 0, 0)
     packed = pl.pallas_call(

time: 85.6 us -> 82.9 us (0.968)
  Pallas kernels: 43 us -> 40.3 us
    pallas_call x3, Pallas kernels: 28.7 us -> 26 us  [attend(): pl.pallas_call(functools.partial(attention_kernel, first, last, stage), o...]
  transfers between devices with their start and end apart: 7 -> 7, of which waited for: 3 -> 3; matrix products, arithmetic and copies ran while one was open for 0% -> 0% of each run, Pallas kernels for 46% -> 44%
where the time goes in v4:
time: 82.9 us; the launch traced here: 82.5 us
  Pallas kernels  40.3 us (49%)
  starting transfers between devices  29.5 us (36%)
  blocking collectives  7.63 us (9%)
  waiting for transfers between devices  4.29 us (5%)
    pallas_call x3, Pallas kernels, attend(): pl.pallas_call(functools.partial(attention_kernel, first, last, stage), o...  26 us
    pallas_call x1, Pallas kernels, body(): pl.pallas_call(prologue_kernel, out_shape=[near_shape((8, TOK), F32), far...  9.49 us
    all_gather x1, blocking collectives, body(): lax.all_gather(key_part, 'head')  7.63 us
    all_to_all x1, starting transfers between devices, body(): recv_mine = lax.all_to_all(payload, 'ctx', 0, 0)  7.6 us
    all_to_all x1, starting transfers between devices, body(): summed = lax.all_to_all(packed, 'ctx', 0, 0)  6.67 us
    ppermute x1, starting transfers between devices, body(): lax.ppermute(send_2, 'dp', [(i, n_dp - 1 - i) for i in range(n_dp)])  5.48 us
    all_to_all x1, starting transfers between devices, body(): weight_ctx = lax.all_to_all(parts, 'ctx', 0, 0)  4.56 us
    ppermute x1, starting transfers between devices, body(): recv_1 = lax.ppermute(send_1, 'dp', [(i, i ^ 1) for i in range(n_dp)])  3.08 us
  transfers between devices with their start and end apart: 7, of which 3 were waited for; matrix products, arithmetic and copies ran while one was open for 0% of the time, Pallas kernels for 44%

profile of v4, /device:TPU:1, one launch (start us, length us, event | category | flops | bytes accessed | tf_op | source)
XLA Modules:
  0.0 82.5 jit_solution(3433848874772318636)
XLA Ops:
  0.6 2.1 %shard_map.94 = bf16[16,160,128]{2,1,0:T(8,128)(2,1)} custom-call(bf16[288,128]{1,0:T(8,128)(2,1)} %bitcast.23, s32[1,128]{1,0:T(1,128)} %rest_1_.5), custom_call_target="tpu_custom_call" | custom-call | tf_op jit(solution)/shard_map/pallas_call | solution.py:356
  2.7 7.6 %all-to-all-start = ((bf16[16,160,128]{2,1,0:T(8,128)(2,1)}), bf16[16,160,128]{2,1,0:T(8,128)(2,1)S(1)}, u32[]{:S(2)}, u32[]{:S(2)}) async-start(bf16[16,160,128]{2,1,0:T(8,128)(2,1)} %shard_map.94), calls=%async_computation | async-start | bytes 1310720 | tf_op jit(solution)/shard_map/all_to_all | solution.py:371
  10.3 9.5 %shard_map.95 = (f32[8,128]{1,0:T(8,128)S(1)}, bf16[16,256,128]{2,1,0:T(8,128)(2,1)}, bf16[16,256,128]{2,1,0:T(8,128)(2,1)}, f32[16,128]{1,0:T(8,128)}, f32[288,...) custom-call(bf16[2048,128]{1,0:T(8,128)(2,1)} %bitcast.22, ...), custom_call_target="tpu_custom_call" | custom-call | flops 996147200 | bytes 8388608 | tf_op jit(solution)/shard_map/pallas_call | solution.py:374
  19.8 2.1 %all-to-all-done.rest_0_ = bf16[16,160,128]{2,1,0:T(8,128)(2,1)S(1)} async-done(((bf16[16,160,128]{2,1,0:T(8,128)(2,1)}), bf16[16,160,128]{2,1,0:T(8,128)(2,1)S(1)}, u32[]{:S(2)}, u32[]{:S(2)}) %all-to-all-start) | async-done | bytes 655392 | tf_op jit(solution)/shard_map/all_to_all | solution.py:371
  21.9 4.6 %all-to-all-start.1 = ((bf16[16,4,64,128]{3,2,1,0:T(8,128)(2,1)}), bf16[16,4,64,128]{3,2,1,0:T(8,128)(2,1)S(1)}, u32[]{:S(2)}, u32[]{:S(2)}) async-start(bf16[16,4,64,128]{3,2,1,0:T(8,128)(2,1)} %get-tuple-element.48), calls=%async_computation.1 | async-start | bytes 2097152 | tf_op jit(solution)/shard_map/all_to_all | solution.py:471
  26.5 1.8 %collective-permute-start = (bf16[16,160,128]{2,1,0:T(8,128)(2,1)S(1)}, bf16[16,160,128]{2,1,0:T(8,128)(2,1)S(1)}, u32[]{:S(2)}, u32[]{:S(2)}) collective-permute-start(bf16[16,160,128]{2,1,0:T(8,128)(2,1)S(1)} %all-to-all-done.rest_0_), channel_id=1, source_target_pairs={{0,1},{1,0},{2,3},{3,2},{4,5},{5,4},{6,7},{7,6},{8,9},{9,8},{10,11... | collective-permute-start | bytes 1966088 | tf_op jit(solution)/shard_map/ppermute | solution.py:354
  28.2 7.4 %shard_map.96 = (f32[8,288,256]{2,1,0:T(8,128)S(1)}, f32[288,512]{1,0:T(8,128)S(1)}, f32[8,128]{1,0:T(8,128)S(1)}, bf16[16,288,128]{2,1,0:T(8,128)(2,1)S(1)}, f3...) custom-call(bf16[16,160,128]{2,1,0:T(8,128)(2,1)S(1)} %all-to-all-do, ...), custom_call_target="tpu_custom_call" | custom-call | flops 8589934592 | bytes 65536 | tf_op jit(solution)/shard_map/pallas_call | solution.py:434
  35.7 0.0 collective-permute-done.rest_0_
  35.7 11.3 %shard_map.97 = (f32[8,288,256]{2,1,0:T(8,128)S(1)}, bf16[288,1024]{1,0:T(8,128)(2,1)}, f32[8,128]{1,0:T(8,128)S(1)}) custom-call(bf16[16,160,128]{2,1,0:T(8,128)(2,1)S(1)} %collective-permute-done.rest_0_, s32[1,128]{1,0:T(1,128)} %rest_1_.5, bf16[16,288,128]{2,1,0:T(8,128)(2,1)S(1)} %get-tuple-element.34.rest_2_, ...), custom_call_target="tpu_custom_call", output_to_operand_aliasing={{0}: (8, {})} | custom-call | flops 8589934592 | bytes 65536 | tf_op jit(solution)/shard_map/pallas_call | solution.py:434
  47.0 0.4 collective-permute-start.1
  47.4 7.3 %shard_map.98 = (bf16[16,288,128]{2,1,0:T(8,128)(2,1)}, f32[288,512]{1,0:T(8,128)S(1)}, f32[8,128]{1,0:T(8,128)}) custom-call(bf16[16,160,128]{2,1,0:T(8,128)(2,1)S(1)} %all-to-all-done.rest_0_, s32[1,128]{1,0:T(1,128)} %rest_1_.5, bf16[16,288,128]{2,1,0:T(8,128)(2,1)S(1)} %get-tuple-element.34.rest_2_, f32[16,128]{1,0:T(8,128)S(1)} %get-tuple-element.35.rest_3_, ...), custom_call_target="tpu_custom_call" | custom-call | flops 8589934592 | bytes 65536 | tf_op jit(solution)/shard_map/pallas_call | solution.py:434
  54.7 0.0 all-to-all-done.1.after.recv
  54.7 0.0 collective-permute-done.1.recv
  54.7 1.1 %shard_map.99.after = bf16[16,144,128]{2,1,0:T(8,128)(2,1)} custom-call(f32[288,512]{1,0:T(8,128)S(1)} %get-tuple-element.45.mine_1, f32[288,512]{1,0:T(8,128)S(1)} %get-tuple-element.46.mine_2, bf16[288,1024]{1,0:T(8,128)(2,1)S(1)} %collective-permute-done.1.recv, bf16[16,4,64,128]{3,2,1,0:T(8,128)(2,1)S(1)} %all-to-all-done.1.after.recv), custom_call_target="tpu_custom_call" | custom-call | tf_op jit(solution)/shard_map/pallas_call | solution.py:472
  55.8 6.7 %all-to-all-start.2 = ((bf16[16,144,128]{2,1,0:T(8,128)(2,1)}), bf16[16,144,128]{2,1,0:T(8,128)(2,1)S(1)}, u32[]{:S(2)}, u32[]{:S(2)}) async-start(bf16[16,144,128]{2,1,0:T(8,128)(2,1)} %shard_map.99.after), calls=%async_computation.2 | async-start | bytes 1179648 | tf_op jit(solution)/shard_map/all_to_all | solution.py:479
  62.5 0.2 shard_map.102
  62.6 3.1 %collective-permute-start.2 = (bf16[2,64,128]{2,1,0:T(8,128)(2,1)S(1)}, bf16[2,64,128]{2,1,0:T(8,128)(2,1)S(1)}, u32[]{:S(2)}, u32[]{:S(2)}) collective-permute-start(bf16[2,64,128]{2,1,0:T(8,128)(2,1)S(1)} %get-tuple-element.50), channel_id=1, source_target_pairs={{0,64},{64,0},{128,192},{192,128},{1,65},{65,1},{129,193},{193,129... | collective-permute-start | bytes 98312 | tf_op jit(solution)/shard_map/ppermute | solution.py:493
  65.7 1.3 %collective-permute-done.2.recv = bf16[2,64,128]{2,1,0:T(8,128)(2,1)S(1)} collective-permute-done((bf16[2,64,128]{2,1,0:T(8,128)(2,1)S(1)}, bf16[2,64,128]{2,1,0:T(8,128)(2,1)S(1)}, u32[]{:S(2)}, u32[]{:S(2)}) %collective-permute-start.2) | collective-permute-done | bytes 32800 | tf_op jit(solution)/shard_map/ppermute | solution.py:493
  67.0 5.5 %collective-permute-start.3 = (bf16[64,128]{1,0:T(8,128)(2,1)S(1)}, bf16[64,128]{1,0:T(8,128)(2,1)S(1)}, u32[]{:S(2)}, u32[]{:S(2)}) collective-permute-start(bf16[64,128]{1,0:T(8,128)(2,1)S(1)} %get-tuple-element.52), channel_id=1, source_target_pairs={{0,192},{64,128},{128,64},{192,0},{1,193},{65,129},{129,65},{193,1... | collective-permute-start | bytes 49160 | tf_op jit(solution)/shard_map/ppermute | solution.py:502
  72.5 0.9 %all-to-all-done.2.recv = bf16[16,144,128]{2,1,0:T(8,128)(2,1)S(1)} async-done(((bf16[16,144,128]{2,1,0:T(8,128)(2,1)}), bf16[16,144,128]{2,1,0:T(8,128)(2,1)S(1)}, u32[]{:S(2)}, u32[]{:S(2)}) %all-to-all-start.2) | async-done | bytes 589856 | tf_op jit(solution)/shard_map/all_to_all | solution.py:479
  73.4 0.1 shard_map.100.after
  73.5 7.6 %all-gather = bf16[576,128]{1,0:T(8,128)(2,1)S(1)} all-gather(bf16[144,128]{1,0:T(8,128)(2,1)S(1)} %shard_map.100.after), channel_id=2, replica_groups=mesh['dp'=4,'ctx'=16,'head'=4] {'head'}, dimensions={0}, use_global_device_ids=true | all-gather | bytes 184320 | tf_op jit(solution)/shard_map/all_gather | solution.py:525
  81.1 0.8 shard_map.101
  81.9 0.0 collective-permute-done.3.weight_recv
  81.9 0.6 shard_map.104
  (1 shorter events, 0.0 us)
Async XLA Ops:
  2.7 19.2 %all-to-all-start = ((bf16[16,160,128]{2,1,0:T(8,128)(2,1)}), bf16[16,160,128]{2,1,0:T(8,128)(2,1)S(1)}, u32[]{:S(2)}, u32[]{:S(2)}) async-start(bf16[16,160,128]{2,1,0:T(8,128)(2,1)} %shard_map.94), calls=%async_computation | async-start | bytes 1310720 | tf_op jit(solution)/shard_map/all_to_all | solution.py:371
  21.9 32.8 %all-to-all-start.1 = ((bf16[16,4,64,128]{3,2,1,0:T(8,128)(2,1)}), bf16[16,4,64,128]{3,2,1,0:T(8,128)(2,1)S(1)}, u32[]{:S(2)}, u32[]{:S(2)}) async-start(bf16[16,4,64,128]{3,2,1,0:T(8,128)(2,1)} %get-tuple-element.48), calls=%async_computation.1 | async-start | bytes 2097152 | tf_op jit(solution)/shard_map/all_to_all | solution.py:471
  26.5 9.2 %collective-permute-start = (bf16[16,160,128]{2,1,0:T(8,128)(2,1)S(1)}, bf16[16,160,128]{2,1,0:T(8,128)(2,1)S(1)}, u32[]{:S(2)}, u32[]{:S(2)}) collective-permute-start(bf16[16,160,128]{2,1,0:T(8,128)(2,1)S(1)} %all-to-all-done.rest_0_), channel_id=1, source_target_pairs={{0,1},{1,0},{2,3},{3,2},{4,5},{5,4},{6,7},{7,6},{8,9},{9,8},{10,11... | collective-permute-start | bytes 1966088 | tf_op jit(solution)/shard_map/ppermute | solution.py:354
  47.0 7.7 %collective-permute-start.1 = (bf16[288,1024]{1,0:T(8,128)(2,1)}, bf16[288,1024]{1,0:T(8,128)(2,1)S(1)}, u32[]{:S(2)}, u32[]{:S(2)}) collective-permute-start(bf16[288,1024]{1,0:T(8,128)(2,1)} %get-tuple-element.47), channel_id=1, source_target_pairs={{0,1},{1,0},{2,3},{3,2},{4,5},{5,4},{6,7},{7,6},{8,9},{9,8},{10,11... | collective-permute-start | bytes 1769480 | tf_op jit(solution)/shard_map/ppermute | solution.py:354
  55.8 17.6 %all-to-all-start.2 = ((bf16[16,144,128]{2,1,0:T(8,128)(2,1)}), bf16[16,144,128]{2,1,0:T(8,128)(2,1)S(1)}, u32[]{:S(2)}, u32[]{:S(2)}) async-start(bf16[16,144,128]{2,1,0:T(8,128)(2,1)} %shard_map.99.after), calls=%async_computation.2 | async-start | bytes 1179648 | tf_op jit(solution)/shard_map/all_to_all | solution.py:479
  62.6 4.4 %collective-permute-start.2 = (bf16[2,64,128]{2,1,0:T(8,128)(2,1)S(1)}, bf16[2,64,128]{2,1,0:T(8,128)(2,1)S(1)}, u32[]{:S(2)}, u32[]{:S(2)}) collective-permute-start(bf16[2,64,128]{2,1,0:T(8,128)(2,1)S(1)} %get-tuple-element.50), channel_id=1, source_target_pairs={{0,64},{64,0},{128,192},{192,128},{1,65},{65,1},{129,193},{193,129... | collective-permute-start | bytes 98312 | tf_op jit(solution)/shard_map/ppermute | solution.py:493
  67.0 14.8 %collective-permute-start.3 = (bf16[64,128]{1,0:T(8,128)(2,1)S(1)}, bf16[64,128]{1,0:T(8,128)(2,1)S(1)}, u32[]{:S(2)}, u32[]{:S(2)}) collective-permute-start(bf16[64,128]{1,0:T(8,128)(2,1)S(1)} %get-tuple-element.52), channel_id=1, source_target_pairs={{0,192},{64,128},{128,64},{192,0},{1,193},{65,129},{129,65},{193,1... | collective-permute-start | bytes 49160 | tf_op jit(solution)/shard_map/ppermute | solution.py:502

commit v5 on v4

--- a/solution.py
+++ b/solution.py
@@ -321,15 +321,11 @@
     key_ref[...] = total.astype(BF16)
 
 
-def share_kernel(stay, weight_recv, after, weight_ref, part_s):
-    del after
+def last_kernel(parts, stay, weight_recv, out_ref, weight_ref, part_s):
     part_s[...] = stay[...] + weight_recv[...].astype(F32)
     width, heads = weight_ref.shape[0], weight_ref.shape[1]
     for i in range(width):
         weight_ref[i] = part_s[pl.ds(i, heads, stride=width), :]
-
-
-def last_kernel(parts, out_ref):
     sides = []
     for core in range(2):
         total = parts[core].astype(F32)
@@ -507,22 +503,14 @@
         out_specs=VM,
         compiler_params=vmem(4),
     )(summed)
-    weight_share = pl.pallas_call(
-        share_kernel,
-        out_shape=shape((width, heads, VHEAD), F32),
-        in_specs=[VM] * 2 + [ANY],
-        out_specs=VM,
+    key_grad, weight_share = pl.pallas_call(
+        last_kernel,
+        out_shape=[shape((FULL, TOK), F32), shape((width, heads, VHEAD), F32)],
+        in_specs=[VM] * 3,
+        out_specs=[VM] * 2,
         scratch_shapes=[pltpu.VMEM((heads * width, VHEAD), F32)],
         compiler_params=vmem(2),
-        cost_estimate=cost(1 << 16, 1 << 16),
-    )(stay, recv_2, key_part)
-    key_grad = pl.pallas_call(
-        last_kernel,
-        out_shape=shape((FULL, TOK), F32),
-        in_specs=[VM],
-        out_specs=VM,
-        compiler_params=vmem(2),
-    )(lax.all_gather(key_part, "head"))
+    )(lax.all_gather(key_part, "head"), stay, recv_2)
     return (jnp.transpose(query_grad, (2, 0, 1))[None], key_grad.T[None], weight_share)
 
 

time: 82.9 us -> 82.3 us (level)
  no operation moved by 1% of the time
where the time goes in v5:
time: 82.3 us; the launch traced here: 81.9 us
  Pallas kernels  39.7 us (48%)
  starting transfers between devices  29.5 us (36%)
  blocking collectives  7.63 us (9%)
  waiting for transfers between devices  4.27 us (5%)
    pallas_call x3, Pallas kernels, attend(): pl.pallas_call(functools.partial(attention_kernel, first, last, stage), o...  26 us
    pallas_call x1, Pallas kernels, body(): pl.pallas_call(prologue_kernel, out_shape=[near_shape((8, TOK), F32), far...  9.5 us
    all_gather x1, blocking collectives, body(): lax.all_gather(key_part, 'head')  7.63 us
    all_to_all x1, starting transfers between devices, body(): recv_mine = lax.all_to_all(payload, 'ctx', 0, 0)  7.6 us
    all_to_all x1, starting transfers between devices, body(): summed = lax.all_to_all(packed, 'ctx', 0, 0)  6.67 us
    ppermute x1, starting transfers between devices, body(): lax.ppermute(send_2, 'dp', [(i, n_dp - 1 - i) for i in range(n_dp)])  5.47 us
    all_to_all x1, starting transfers between devices, body(): weight_ctx = lax.all_to_all(parts, 'ctx', 0, 0)  4.57 us
    ppermute x1, starting transfers between devices, body(): recv_1 = lax.ppermute(send_1, 'dp', [(i, i ^ 1) for i in range(n_dp)])  3.08 us
  transfers between devices with their start and end apart: 7, of which 3 were waited for; matrix products, arithmetic and copies ran while one was open for 0% of the time, Pallas kernels for 44%

profile of v5, /device:TPU:1, one launch (start us, length us, event | category | flops | bytes accessed | tf_op | source)
XLA Modules:
  0.0 81.9 jit_solution(1372555376511659992)
XLA Ops:
  0.6 2.1 %shard_map.94 = bf16[16,160,128]{2,1,0:T(8,128)(2,1)} custom-call(bf16[288,128]{1,0:T(8,128)(2,1)} %bitcast.23, s32[1,128]{1,0:T(1,128)} %rest_1_.5), custom_call_target="tpu_custom_call" | custom-call | tf_op jit(solution)/shard_map/pallas_call | solution.py:352
  2.7 7.6 %all-to-all-start = ((bf16[16,160,128]{2,1,0:T(8,128)(2,1)}), bf16[16,160,128]{2,1,0:T(8,128)(2,1)S(1)}, u32[]{:S(2)}, u32[]{:S(2)}) async-start(bf16[16,160,128]{2,1,0:T(8,128)(2,1)} %shard_map.94), calls=%async_computation | async-start | bytes 1310720 | tf_op jit(solution)/shard_map/all_to_all | solution.py:367
  10.3 9.5 %shard_map.95 = (f32[8,128]{1,0:T(8,128)S(1)}, bf16[16,256,128]{2,1,0:T(8,128)(2,1)}, bf16[16,256,128]{2,1,0:T(8,128)(2,1)}, f32[16,128]{1,0:T(8,128)}, f32[288,...) custom-call(bf16[2048,128]{1,0:T(8,128)(2,1)} %bitcast.22, ...), custom_call_target="tpu_custom_call" | custom-call | flops 996147200 | bytes 8388608 | tf_op jit(solution)/shard_map/pallas_call | solution.py:370
  19.8 2.1 %all-to-all-done.rest_0_ = bf16[16,160,128]{2,1,0:T(8,128)(2,1)S(1)} async-done(((bf16[16,160,128]{2,1,0:T(8,128)(2,1)}), bf16[16,160,128]{2,1,0:T(8,128)(2,1)S(1)}, u32[]{:S(2)}, u32[]{:S(2)}) %all-to-all-start) | async-done | bytes 655392 | tf_op jit(solution)/shard_map/all_to_all | solution.py:367
  21.9 4.6 %all-to-all-start.1 = ((bf16[16,4,64,128]{3,2,1,0:T(8,128)(2,1)}), bf16[16,4,64,128]{3,2,1,0:T(8,128)(2,1)S(1)}, u32[]{:S(2)}, u32[]{:S(2)}) async-start(bf16[16,4,64,128]{3,2,1,0:T(8,128)(2,1)} %get-tuple-element.50), calls=%async_computation.1 | async-start | bytes 2097152 | tf_op jit(solution)/shard_map/all_to_all | solution.py:467
  26.5 1.8 %collective-permute-start = (bf16[16,160,128]{2,1,0:T(8,128)(2,1)S(1)}, bf16[16,160,128]{2,1,0:T(8,128)(2,1)S(1)}, u32[]{:S(2)}, u32[]{:S(2)}) collective-permute-start(bf16[16,160,128]{2,1,0:T(8,128)(2,1)S(1)} %all-to-all-done.rest_0_), channel_id=1, source_target_pairs={{0,1},{1,0},{2,3},{3,2},{4,5},{5,4},{6,7},{7,6},{8,9},{9,8},{10,11... | collective-permute-start | bytes 1966088 | tf_op jit(solution)/shard_map/ppermute | solution.py:350
  28.3 7.4 %shard_map.96 = (f32[8,288,256]{2,1,0:T(8,128)S(1)}, f32[288,512]{1,0:T(8,128)S(1)}, f32[8,128]{1,0:T(8,128)S(1)}, bf16[16,288,128]{2,1,0:T(8,128)(2,1)S(1)}, f3...) custom-call(bf16[16,160,128]{2,1,0:T(8,128)(2,1)S(1)} %all-to-all-do, ...), custom_call_target="tpu_custom_call" | custom-call | flops 8589934592 | bytes 65536 | tf_op jit(solution)/shard_map/pallas_call | solution.py:430
  35.7 0.0 collective-permute-done.rest_0_
  35.7 11.3 %shard_map.97 = (f32[8,288,256]{2,1,0:T(8,128)S(1)}, bf16[288,1024]{1,0:T(8,128)(2,1)}, f32[8,128]{1,0:T(8,128)S(1)}) custom-call(bf16[16,160,128]{2,1,0:T(8,128)(2,1)S(1)} %collective-permute-done.rest_0_, s32[1,128]{1,0:T(1,128)} %rest_1_.5, bf16[16,288,128]{2,1,0:T(8,128)(2,1)S(1)} %get-tuple-element.36.rest_2_, ...), custom_call_target="tpu_custom_call", output_to_operand_aliasing={{0}: (8, {})} | custom-call | flops 8589934592 | bytes 65536 | tf_op jit(solution)/shard_map/pallas_call | solution.py:430
  47.0 0.4 collective-permute-start.1
  47.4 7.3 %shard_map.98 = (bf16[16,288,128]{2,1,0:T(8,128)(2,1)}, f32[288,512]{1,0:T(8,128)S(1)}, f32[8,128]{1,0:T(8,128)}) custom-call(bf16[16,160,128]{2,1,0:T(8,128)(2,1)S(1)} %all-to-all-done.rest_0_, s32[1,128]{1,0:T(1,128)} %rest_1_.5, bf16[16,288,128]{2,1,0:T(8,128)(2,1)S(1)} %get-tuple-element.36.rest_2_, f32[16,128]{1,0:T(8,128)S(1)} %get-tuple-element.37.rest_3_, ...), custom_call_target="tpu_custom_call" | custom-call | flops 8589934592 | bytes 65536 | tf_op jit(solution)/shard_map/pallas_call | solution.py:430
  54.7 0.0 all-to-all-done.1.after.recv
  54.7 0.0 collective-permute-done.1.recv
  54.7 1.1 %shard_map.99.after = bf16[16,144,128]{2,1,0:T(8,128)(2,1)} custom-call(f32[288,512]{1,0:T(8,128)S(1)} %get-tuple-element.47.mine_1, f32[288,512]{1,0:T(8,128)S(1)} %get-tuple-element.48.mine_2, bf16[288,1024]{1,0:T(8,128)(2,1)S(1)} %collective-permute-done.1.recv, bf16[16,4,64,128]{3,2,1,0:T(8,128)(2,1)S(1)} %all-to-all-done.1.after.recv), custom_call_target="tpu_custom_call" | custom-call | tf_op jit(solution)/shard_map/pallas_call | solution.py:468
  55.8 6.7 %all-to-all-start.2 = ((bf16[16,144,128]{2,1,0:T(8,128)(2,1)}), bf16[16,144,128]{2,1,0:T(8,128)(2,1)S(1)}, u32[]{:S(2)}, u32[]{:S(2)}) async-start(bf16[16,144,128]{2,1,0:T(8,128)(2,1)} %shard_map.99.after), calls=%async_computation.2 | async-start | bytes 1179648 | tf_op jit(solution)/shard_map/all_to_all | solution.py:475
  62.5 0.2 shard_map.101
  62.6 3.1 %collective-permute-start.2 = (bf16[2,64,128]{2,1,0:T(8,128)(2,1)S(1)}, bf16[2,64,128]{2,1,0:T(8,128)(2,1)S(1)}, u32[]{:S(2)}, u32[]{:S(2)}) collective-permute-start(bf16[2,64,128]{2,1,0:T(8,128)(2,1)S(1)} %get-tuple-element.52), channel_id=1, source_target_pairs={{0,64},{64,0},{128,192},{192,128},{1,65},{65,1},{129,193},{193,129... | collective-permute-start | bytes 98312 | tf_op jit(solution)/shard_map/ppermute | solution.py:489
  65.7 1.3 %collective-permute-done.2.recv = bf16[2,64,128]{2,1,0:T(8,128)(2,1)S(1)} collective-permute-done((bf16[2,64,128]{2,1,0:T(8,128)(2,1)S(1)}, bf16[2,64,128]{2,1,0:T(8,128)(2,1)S(1)}, u32[]{:S(2)}, u32[]{:S(2)}) %collective-permute-start.2) | collective-permute-done | bytes 32800 | tf_op jit(solution)/shard_map/ppermute | solution.py:489
  67.0 5.5 %collective-permute-start.3 = (bf16[64,128]{1,0:T(8,128)(2,1)S(1)}, bf16[64,128]{1,0:T(8,128)(2,1)S(1)}, u32[]{:S(2)}, u32[]{:S(2)}) collective-permute-start(bf16[64,128]{1,0:T(8,128)(2,1)S(1)} %get-tuple-element.54), channel_id=1, source_target_pairs={{0,192},{64,128},{128,64},{192,0},{1,193},{65,129},{129,65},{193,1... | collective-permute-start | bytes 49160 | tf_op jit(solution)/shard_map/ppermute | solution.py:498
  72.5 0.9 %all-to-all-done.2.recv = bf16[16,144,128]{2,1,0:T(8,128)(2,1)S(1)} async-done(((bf16[16,144,128]{2,1,0:T(8,128)(2,1)}), bf16[16,144,128]{2,1,0:T(8,128)(2,1)S(1)}, u32[]{:S(2)}, u32[]{:S(2)}) %all-to-all-start.2) | async-done | bytes 589856 | tf_op jit(solution)/shard_map/all_to_all | solution.py:475
  73.4 0.1 shard_map.100
  73.5 7.6 %all-gather = bf16[576,128]{1,0:T(8,128)(2,1)S(1)} all-gather(bf16[144,128]{1,0:T(8,128)(2,1)S(1)} %shard_map.100), channel_id=2, replica_groups=mesh['dp'=4,'ctx'=16,'head'=4] {'head'}, dimensions={0}, use_global_device_ids=true | all-gather | bytes 184320 | tf_op jit(solution)/shard_map/all_gather | solution.py:513
  81.1 0.0 collective-permute-done.3.weight_recv
  81.1 0.8 shard_map.103
  (1 shorter events, 0.0 us)
Async XLA Ops:
  2.7 19.2 %all-to-all-start = ((bf16[16,160,128]{2,1,0:T(8,128)(2,1)}), bf16[16,160,128]{2,1,0:T(8,128)(2,1)S(1)}, u32[]{:S(2)}, u32[]{:S(2)}) async-start(bf16[16,160,128]{2,1,0:T(8,128)(2,1)} %shard_map.94), calls=%async_computation | async-start | bytes 1310720 | tf_op jit(solution)/shard_map/all_to_all | solution.py:367
  21.9 32.8 %all-to-all-start.1 = ((bf16[16,4,64,128]{3,2,1,0:T(8,128)(2,1)}), bf16[16,4,64,128]{3,2,1,0:T(8,128)(2,1)S(1)}, u32[]{:S(2)}, u32[]{:S(2)}) async-start(bf16[16,4,64,128]{3,2,1,0:T(8,128)(2,1)} %get-tuple-element.50), calls=%async_computation.1 | async-start | bytes 2097152 | tf_op jit(solution)/shard_map/all_to_all | solution.py:467
  26.5 9.2 %collective-permute-start = (bf16[16,160,128]{2,1,0:T(8,128)(2,1)S(1)}, bf16[16,160,128]{2,1,0:T(8,128)(2,1)S(1)}, u32[]{:S(2)}, u32[]{:S(2)}) collective-permute-start(bf16[16,160,128]{2,1,0:T(8,128)(2,1)S(1)} %all-to-all-done.rest_0_), channel_id=1, source_target_pairs={{0,1},{1,0},{2,3},{3,2},{4,5},{5,4},{6,7},{7,6},{8,9},{9,8},{10,11... | collective-permute-start | bytes 1966088 | tf_op jit(solution)/shard_map/ppermute | solution.py:350
  47.0 7.7 %collective-permute-start.1 = (bf16[288,1024]{1,0:T(8,128)(2,1)}, bf16[288,1024]{1,0:T(8,128)(2,1)S(1)}, u32[]{:S(2)}, u32[]{:S(2)}) collective-permute-start(bf16[288,1024]{1,0:T(8,128)(2,1)} %get-tuple-element.49), channel_id=1, source_target_pairs={{0,1},{1,0},{2,3},{3,2},{4,5},{5,4},{6,7},{7,6},{8,9},{9,8},{10,11... | collective-permute-start | bytes 1769480 | tf_op jit(solution)/shard_map/ppermute | solution.py:350
  55.8 17.6 %all-to-all-start.2 = ((bf16[16,144,128]{2,1,0:T(8,128)(2,1)}), bf16[16,144,128]{2,1,0:T(8,128)(2,1)S(1)}, u32[]{:S(2)}, u32[]{:S(2)}) async-start(bf16[16,144,128]{2,1,0:T(8,128)(2,1)} %shard_map.99.after), calls=%async_computation.2 | async-start | bytes 1179648 | tf_op jit(solution)/shard_map/all_to_all | solution.py:475
  62.6 4.4 %collective-permute-start.2 = (bf16[2,64,128]{2,1,0:T(8,128)(2,1)S(1)}, bf16[2,64,128]{2,1,0:T(8,128)(2,1)S(1)}, u32[]{:S(2)}, u32[]{:S(2)}) collective-permute-start(bf16[2,64,128]{2,1,0:T(8,128)(2,1)S(1)} %get-tuple-element.52), channel_id=1, source_target_pairs={{0,64},{64,0},{128,192},{192,128},{1,65},{65,1},{129,193},{193,129... | collective-permute-start | bytes 98312 | tf_op jit(solution)/shard_map/ppermute | solution.py:489
  67.0 14.1 %collective-permute-start.3 = (bf16[64,128]{1,0:T(8,128)(2,1)S(1)}, bf16[64,128]{1,0:T(8,128)(2,1)S(1)}, u32[]{:S(2)}, u32[]{:S(2)}) collective-permute-start(bf16[64,128]{1,0:T(8,128)(2,1)S(1)} %get-tuple-element.54), channel_id=1, source_target_pairs={{0,192},{64,128},{128,64},{192,0},{1,193},{65,129},{129,65},{193,1... | collective-permute-start | bytes 49160 | tf_op jit(solution)/shard_map/ppermute | solution.py:498

commit v6 on v5

--- a/solution.py
+++ b/solution.py
@@ -264,9 +264,9 @@
 
     for lo in range(0, count * HALF, TOK):
         keys_t[:, lo : lo + TOK] = key_s[lo : lo + TOK, :].T
-    steps = 4 if stage else 1
+    steps = 2 if stage else 1
     for i in range(steps):
-        for copy in groups[i]:
+        for copy in groups[2 * i] + groups[2 * i + 1]:
             copy.wait()
         each = heads // 2 // steps
         lax.fori_loop(each * i, each * i + each, one, 0, unroll=each)

time: 82.3 us -> 82.5 us (level)
  no operation moved by 1% of the time
where the time goes in v6:
time: 82.5 us; the launch traced here: 82 us
  Pallas kernels  39.8 us (48%)
  starting transfers between devices  29.5 us (36%)
  blocking collectives  7.62 us (9%)
  waiting for transfers between devices  4.28 us (5%)
    pallas_call x3, Pallas kernels, attend(): pl.pallas_call(functools.partial(attention_kernel, first, last, stage), o...  26.2 us
    pallas_call x1, Pallas kernels, body(): pl.pallas_call(prologue_kernel, out_shape=[near_shape((8, TOK), F32), far...  9.5 us
    all_gather x1, blocking collectives, body(): lax.all_gather(key_part, 'head')  7.62 us
    all_to_all x1, starting transfers between devices, body(): recv_mine = lax.all_to_all(payload, 'ctx', 0, 0)  7.6 us
    all_to_all x1, starting transfers between devices, body(): summed = lax.all_to_all(packed, 'ctx', 0, 0)  6.67 us
    ppermute x1, starting transfers between devices, body(): lax.ppermute(send_2, 'dp', [(i, n_dp - 1 - i) for i in range(n_dp)])  5.47 us
    all_to_all x1, starting transfers between devices, body(): weight_ctx = lax.all_to_all(parts, 'ctx', 0, 0)  4.57 us
    ppermute x1, starting transfers between devices, body(): recv_1 = lax.ppermute(send_1, 'dp', [(i, i ^ 1) for i in range(n_dp)])  3.08 us
  transfers between devices with their start and end apart: 7, of which 3 were waited for; matrix products, arithmetic and copies ran while one was open for 0% of the time, Pallas kernels for 44%

profile of v6, /device:TPU:1, one launch (start us, length us, event | category | flops | bytes accessed | tf_op | source)
XLA Modules:
  0.0 82.0 jit_solution(10548099157081545366)
XLA Ops:
  0.6 2.1 %shard_map.94 = bf16[16,160,128]{2,1,0:T(8,128)(2,1)} custom-call(bf16[288,128]{1,0:T(8,128)(2,1)} %bitcast.23, s32[1,128]{1,0:T(1,128)} %rest_1_.5), custom_call_target="tpu_custom_call" | custom-call | tf_op jit(solution)/shard_map/pallas_call | solution.py:352
  2.7 7.6 %all-to-all-start = ((bf16[16,160,128]{2,1,0:T(8,128)(2,1)}), bf16[16,160,128]{2,1,0:T(8,128)(2,1)S(1)}, u32[]{:S(2)}, u32[]{:S(2)}) async-start(bf16[16,160,128]{2,1,0:T(8,128)(2,1)} %shard_map.94), calls=%async_computation | async-start | bytes 1310720 | tf_op jit(solution)/shard_map/all_to_all | solution.py:367
  10.3 9.5 %shard_map.95 = (f32[8,128]{1,0:T(8,128)S(1)}, bf16[16,256,128]{2,1,0:T(8,128)(2,1)}, bf16[16,256,128]{2,1,0:T(8,128)(2,1)}, f32[16,128]{1,0:T(8,128)}, f32[288,...) custom-call(bf16[2048,128]{1,0:T(8,128)(2,1)} %bitcast.22, ...), custom_call_target="tpu_custom_call" | custom-call | flops 996147200 | bytes 8388608 | tf_op jit(solution)/shard_map/pallas_call | solution.py:370
  19.8 2.1 %all-to-all-done.rest_0_ = bf16[16,160,128]{2,1,0:T(8,128)(2,1)S(1)} async-done(((bf16[16,160,128]{2,1,0:T(8,128)(2,1)}), bf16[16,160,128]{2,1,0:T(8,128)(2,1)S(1)}, u32[]{:S(2)}, u32[]{:S(2)}) %all-to-all-start) | async-done | bytes 655392 | tf_op jit(solution)/shard_map/all_to_all | solution.py:367
  21.9 4.6 %all-to-all-start.1 = ((bf16[16,4,64,128]{3,2,1,0:T(8,128)(2,1)}), bf16[16,4,64,128]{3,2,1,0:T(8,128)(2,1)S(1)}, u32[]{:S(2)}, u32[]{:S(2)}) async-start(bf16[16,4,64,128]{3,2,1,0:T(8,128)(2,1)} %get-tuple-element.50), calls=%async_computation.1 | async-start | bytes 2097152 | tf_op jit(solution)/shard_map/all_to_all | solution.py:467
  26.5 1.8 %collective-permute-start = (bf16[16,160,128]{2,1,0:T(8,128)(2,1)S(1)}, bf16[16,160,128]{2,1,0:T(8,128)(2,1)S(1)}, u32[]{:S(2)}, u32[]{:S(2)}) collective-permute-start(bf16[16,160,128]{2,1,0:T(8,128)(2,1)S(1)} %all-to-all-done.rest_0_), channel_id=1, source_target_pairs={{0,1},{1,0},{2,3},{3,2},{4,5},{5,4},{6,7},{7,6},{8,9},{9,8},{10,11... | collective-permute-start | bytes 1966088 | tf_op jit(solution)/shard_map/ppermute | solution.py:350
  28.3 7.6 %shard_map.96 = (f32[8,288,256]{2,1,0:T(8,128)S(1)}, f32[288,512]{1,0:T(8,128)S(1)}, f32[8,128]{1,0:T(8,128)S(1)}, bf16[16,288,128]{2,1,0:T(8,128)(2,1)S(1)}, f3...) custom-call(bf16[16,160,128]{2,1,0:T(8,128)(2,1)S(1)} %all-to-all-do, ...), custom_call_target="tpu_custom_call" | custom-call | flops 8589934592 | bytes 65536 | tf_op jit(solution)/shard_map/pallas_call | solution.py:430
  35.8 0.0 collective-permute-done.rest_0_
  35.8 11.3 %shard_map.97 = (f32[8,288,256]{2,1,0:T(8,128)S(1)}, bf16[288,1024]{1,0:T(8,128)(2,1)}, f32[8,128]{1,0:T(8,128)S(1)}) custom-call(bf16[16,160,128]{2,1,0:T(8,128)(2,1)S(1)} %collective-permute-done.rest_0_, s32[1,128]{1,0:T(1,128)} %rest_1_.5, bf16[16,288,128]{2,1,0:T(8,128)(2,1)S(1)} %get-tuple-element.36.rest_2_, ...), custom_call_target="tpu_custom_call", output_to_operand_aliasing={{0}: (8, {})} | custom-call | flops 8589934592 | bytes 65536 | tf_op jit(solution)/shard_map/pallas_call | solution.py:430
  47.2 0.4 collective-permute-start.1
  47.6 7.3 %shard_map.98 = (bf16[16,288,128]{2,1,0:T(8,128)(2,1)}, f32[288,512]{1,0:T(8,128)S(1)}, f32[8,128]{1,0:T(8,128)}) custom-call(bf16[16,160,128]{2,1,0:T(8,128)(2,1)S(1)} %all-to-all-done.rest_0_, s32[1,128]{1,0:T(1,128)} %rest_1_.5, bf16[16,288,128]{2,1,0:T(8,128)(2,1)S(1)} %get-tuple-element.36.rest_2_, f32[16,128]{1,0:T(8,128)S(1)} %get-tuple-element.37.rest_3_, ...), custom_call_target="tpu_custom_call" | custom-call | flops 8589934592 | bytes 65536 | tf_op jit(solution)/shard_map/pallas_call | solution.py:430
  54.8 0.0 all-to-all-done.1.after.recv
  54.8 0.0 collective-permute-done.1.recv
  54.8 1.1 %shard_map.99.after = bf16[16,144,128]{2,1,0:T(8,128)(2,1)} custom-call(f32[288,512]{1,0:T(8,128)S(1)} %get-tuple-element.47.mine_1, f32[288,512]{1,0:T(8,128)S(1)} %get-tuple-element.48.mine_2, bf16[288,1024]{1,0:T(8,128)(2,1)S(1)} %collective-permute-done.1.recv, bf16[16,4,64,128]{3,2,1,0:T(8,128)(2,1)S(1)} %all-to-all-done.1.after.recv), custom_call_target="tpu_custom_call" | custom-call | tf_op jit(solution)/shard_map/pallas_call | solution.py:468
  55.9 6.7 %all-to-all-start.2 = ((bf16[16,144,128]{2,1,0:T(8,128)(2,1)}), bf16[16,144,128]{2,1,0:T(8,128)(2,1)S(1)}, u32[]{:S(2)}, u32[]{:S(2)}) async-start(bf16[16,144,128]{2,1,0:T(8,128)(2,1)} %shard_map.99.after), calls=%async_computation.2 | async-start | bytes 1179648 | tf_op jit(solution)/shard_map/all_to_all | solution.py:475
  62.6 0.2 shard_map.101
  62.8 3.1 %collective-permute-start.2 = (bf16[2,64,128]{2,1,0:T(8,128)(2,1)S(1)}, bf16[2,64,128]{2,1,0:T(8,128)(2,1)S(1)}, u32[]{:S(2)}, u32[]{:S(2)}) collective-permute-start(bf16[2,64,128]{2,1,0:T(8,128)(2,1)S(1)} %get-tuple-element.52), channel_id=1, source_target_pairs={{0,64},{64,0},{128,192},{192,128},{1,65},{65,1},{129,193},{193,129... | collective-permute-start | bytes 98312 | tf_op jit(solution)/shard_map/ppermute | solution.py:489
  65.9 1.3 %collective-permute-done.2.recv = bf16[2,64,128]{2,1,0:T(8,128)(2,1)S(1)} collective-permute-done((bf16[2,64,128]{2,1,0:T(8,128)(2,1)S(1)}, bf16[2,64,128]{2,1,0:T(8,128)(2,1)S(1)}, u32[]{:S(2)}, u32[]{:S(2)}) %collective-permute-start.2) | collective-permute-done | bytes 32800 | tf_op jit(solution)/shard_map/ppermute | solution.py:489
  67.2 5.5 %collective-permute-start.3 = (bf16[64,128]{1,0:T(8,128)(2,1)S(1)}, bf16[64,128]{1,0:T(8,128)(2,1)S(1)}, u32[]{:S(2)}, u32[]{:S(2)}) collective-permute-start(bf16[64,128]{1,0:T(8,128)(2,1)S(1)} %get-tuple-element.54), channel_id=1, source_target_pairs={{0,192},{64,128},{128,64},{192,0},{1,193},{65,129},{129,65},{193,1... | collective-permute-start | bytes 49160 | tf_op jit(solution)/shard_map/ppermute | solution.py:498
  72.6 0.9 %all-to-all-done.2.recv = bf16[16,144,128]{2,1,0:T(8,128)(2,1)S(1)} async-done(((bf16[16,144,128]{2,1,0:T(8,128)(2,1)}), bf16[16,144,128]{2,1,0:T(8,128)(2,1)S(1)}, u32[]{:S(2)}, u32[]{:S(2)}) %all-to-all-start.2) | async-done | bytes 589856 | tf_op jit(solution)/shard_map/all_to_all | solution.py:475
  73.5 0.1 shard_map.100
  73.6 7.6 %all-gather = bf16[576,128]{1,0:T(8,128)(2,1)S(1)} all-gather(bf16[144,128]{1,0:T(8,128)(2,1)S(1)} %shard_map.100), channel_id=2, replica_groups=mesh['dp'=4,'ctx'=16,'head'=4] {'head'}, dimensions={0}, use_global_device_ids=true | all-gather | bytes 184320 | tf_op jit(solution)/shard_map/all_gather | solution.py:513
  81.2 0.0 collective-permute-done.3.weight_recv
  81.2 0.8 shard_map.103
  (1 shorter events, 0.0 us)
Async XLA Ops:
  2.7 19.2 %all-to-all-start = ((bf16[16,160,128]{2,1,0:T(8,128)(2,1)}), bf16[16,160,128]{2,1,0:T(8,128)(2,1)S(1)}, u32[]{:S(2)}, u32[]{:S(2)}) async-start(bf16[16,160,128]{2,1,0:T(8,128)(2,1)} %shard_map.94), calls=%async_computation | async-start | bytes 1310720 | tf_op jit(solution)/shard_map/all_to_all | solution.py:367
  21.9 32.9 %all-to-all-start.1 = ((bf16[16,4,64,128]{3,2,1,0:T(8,128)(2,1)}), bf16[16,4,64,128]{3,2,1,0:T(8,128)(2,1)S(1)}, u32[]{:S(2)}, u32[]{:S(2)}) async-start(bf16[16,4,64,128]{3,2,1,0:T(8,128)(2,1)} %get-tuple-element.50), calls=%async_computation.1 | async-start | bytes 2097152 | tf_op jit(solution)/shard_map/all_to_all | solution.py:467
  26.5 9.4 %collective-permute-start = (bf16[16,160,128]{2,1,0:T(8,128)(2,1)S(1)}, bf16[16,160,128]{2,1,0:T(8,128)(2,1)S(1)}, u32[]{:S(2)}, u32[]{:S(2)}) collective-permute-start(bf16[16,160,128]{2,1,0:T(8,128)(2,1)S(1)} %all-to-all-done.rest_0_), channel_id=1, source_target_pairs={{0,1},{1,0},{2,3},{3,2},{4,5},{5,4},{6,7},{7,6},{8,9},{9,8},{10,11... | collective-permute-start | bytes 1966088 | tf_op jit(solution)/shard_map/ppermute | solution.py:350
  47.2 7.7 %collective-permute-start.1 = (bf16[288,1024]{1,0:T(8,128)(2,1)}, bf16[288,1024]{1,0:T(8,128)(2,1)S(1)}, u32[]{:S(2)}, u32[]{:S(2)}) collective-permute-start(bf16[288,1024]{1,0:T(8,128)(2,1)} %get-tuple-element.49), channel_id=1, source_target_pairs={{0,1},{1,0},{2,3},{3,2},{4,5},{5,4},{6,7},{7,6},{8,9},{9,8},{10,11... | collective-permute-start | bytes 1769480 | tf_op jit(solution)/shard_map/ppermute | solution.py:350
  55.9 17.6 %all-to-all-start.2 = ((bf16[16,144,128]{2,1,0:T(8,128)(2,1)}), bf16[16,144,128]{2,1,0:T(8,128)(2,1)S(1)}, u32[]{:S(2)}, u32[]{:S(2)}) async-start(bf16[16,144,128]{2,1,0:T(8,128)(2,1)} %shard_map.99.after), calls=%async_computation.2 | async-start | bytes 1179648 | tf_op jit(solution)/shard_map/all_to_all | solution.py:475
  62.8 4.4 %collective-permute-start.2 = (bf16[2,64,128]{2,1,0:T(8,128)(2,1)S(1)}, bf16[2,64,128]{2,1,0:T(8,128)(2,1)S(1)}, u32[]{:S(2)}, u32[]{:S(2)}) collective-permute-start(bf16[2,64,128]{2,1,0:T(8,128)(2,1)S(1)} %get-tuple-element.52), channel_id=1, source_target_pairs={{0,64},{64,0},{128,192},{192,128},{1,65},{65,1},{129,193},{193,129... | collective-permute-start | bytes 98312 | tf_op jit(solution)/shard_map/ppermute | solution.py:489
  67.2 14.1 %collective-permute-start.3 = (bf16[64,128]{1,0:T(8,128)(2,1)S(1)}, bf16[64,128]{1,0:T(8,128)(2,1)S(1)}, u32[]{:S(2)}, u32[]{:S(2)}) collective-permute-start(bf16[64,128]{1,0:T(8,128)(2,1)S(1)} %get-tuple-element.54), channel_id=1, source_target_pairs={{0,192},{64,128},{128,64},{192,0},{1,193},{65,129},{129,65},{193,1... | collective-permute-start | bytes 49160 | tf_op jit(solution)/shard_map/ppermute | solution.py:498
